TPU v7x, 768 devices: a whole 4x8x12 slice. The times are simulated.
768 devices in a mesh: scene: 8 (over x, core), brick: 96 (over y, z).
Axes of the slice: x: 4, y: 8, z: 12, core: 2. Of those that a mesh axis runs over, the one named last changes fastest.
Arguments:
- features: bfloat16 [8, 49152, 64], P('scene', 'brick'), may hold values from -6 to 6
- cotangent: bfloat16 [8, 49152, 64], P('scene', 'brick'), may hold values from -6 to 6
- first_weight: bfloat16 [1728, 64], replicated, may hold values from -0.15625 to 0.15625
- second_weight: bfloat16 [1728, 64], replicated, may hold values from -0.15625 to 0.15625
- send_rows: int32 [8, 12288], P('scene', 'brick'), may hold values from 0 to 512, as said below
- gather_rows: int32 [8, 96000], P('scene', 'brick'), may hold values from 0 to 640, as said below
Outputs:
- output: bfloat16 [8, 49152, 64], P('scene', 'brick')
- grad_input: bfloat16 [8, 49152, 64], P('scene', 'brick')
- grad_first: float32 [1728, 64], replicated
- grad_second: float32 [1728, 64], replicated
Inputs may be any that keep to these rules, and one draw needn't show every extreme that they name: `send_rows`: entries equal to 512 are empty slots; used entries come first in each half and name voxels on the face of active bricks towards that neighbour; in every draw some pair of neighbouring indices sends all 64 rows to each other. Index 0 sends nothing down, the last index nothing up. `gather_rows`: row 640 is the zero row; inactive slots read only it; rows 512 and up read boundary rows in the order of the neighbour's send list. Every index of brick holds exactly one active brick slot, and bricks touch only bricks of the same or an adjacent index.
All inputs are finite; a program needn't handle non-finite values.
Results may differ from a plain program's by a relative error of at most 0.0059.
Values may be sent and summed in bfloat16 or wider, within the bound.
A program may use at most 32 MiB of HBM per device.

v0:
```python
import jax
import jax.numpy as jnp
from jax import lax
from jax.sharding import PartitionSpec as P

EDGE = 8
VOX = 512


def extended(block, sides, width):
    for axis, dim in sides:
        count = lax.axis_size(axis)
        forward = [(i, i + 1) for i in range(count - 1)]
        backward = [(target, source) for source, target in forward]
        low = lax.ppermute(
            lax.slice_in_dim(block, block.shape[dim] - width, None, axis=dim), axis, forward
        )
        high = lax.ppermute(lax.slice_in_dim(block, 0, width, axis=dim), axis, backward)
        block = jnp.concatenate([low, block, high], axis=dim)
    return block


def silu_slope(values):
    sig = jax.nn.sigmoid(values)
    return sig * (1.0 + values * (1.0 - sig))


def outgoing_rows(values, send_list):
    zero_row = jnp.zeros((1, values.shape[1]), values.dtype)
    return jnp.take(jnp.concatenate([values, zero_row], axis=0), send_list, axis=0)


def assemble(values, arrived, gather_list, slot_width):
    zero_row = jnp.zeros((1, values.shape[1]), values.dtype)
    pool = jnp.concatenate(
        [values, arrived[:slot_width], arrived[3 * slot_width :], zero_row], axis=0
    )
    return jnp.take(pool, gather_list, axis=0).reshape(
        -1, EDGE + 2, EDGE + 2, EDGE + 2, values.shape[1]
    )


def window_rows(padded, row_off, col_off, extent):
    slabs = [
        padded[:, row_off : row_off + extent, col_off : col_off + extent, depth : depth + extent, :]
        for depth in range(3)
    ]
    return jnp.concatenate(slabs, axis=-1).reshape(-1, 3 * padded.shape[-1])


def convolve(padded, weight, extent):
    width = padded.shape[-1]
    accumulated = jnp.zeros((padded.shape[0] * extent**3, weight.shape[1]), jnp.float32)
    for row_off in range(3):
        for col_off in range(3):
            start = (row_off * 3 + col_off) * 3 * width
            accumulated = accumulated + jnp.dot(
                window_rows(padded, row_off, col_off, extent),
                weight[start : start + 3 * width],
                preferred_element_type=jnp.float32,
            )
    return accumulated


def weight_gradient(padded, delta_rows):
    pieces = []
    for row_off in range(3):
        for col_off in range(3):
            pieces.append(
                lax.dot_general(
                    window_rows(padded, row_off, col_off, EDGE),
                    delta_rows,
                    (((0,), (0,)), ((), ())),
                    preferred_element_type=jnp.float32,
                )
            )
    return jnp.concatenate(pieces, axis=0)


def flipped(weight):
    width = weight.shape[1]
    return jnp.transpose(weight.reshape(27, width, width)[::-1], (0, 2, 1)).reshape(
        27 * width, width
    )


def shards(features, cotangent, first_weight, second_weight, send_rows, gather_rows):
    local_feat = features[0]
    local_cot = cotangent[0]
    send_list = send_rows[0]
    gather_list = gather_rows[0]
    slot_width = send_list.shape[0] // 2

    def forward_pad(values):
        arrived = extended(outgoing_rows(values, send_list), (("brick", 0),), slot_width)
        return assemble(values, arrived, gather_list, slot_width)

    def delta_pad(values):
        arrived = extended(outgoing_rows(values, send_list), (("brick", 0),), slot_width)
        return assemble(values, arrived, gather_list, slot_width)

    padded_input = forward_pad(local_feat)
    first_pre = convolve(padded_input, first_weight, EDGE)
    first_act = (first_pre * jax.nn.sigmoid(first_pre)).astype(jnp.bfloat16)
    padded_act = forward_pad(first_act)
    second_pre = convolve(padded_act, second_weight, EDGE)
    output = (second_pre * jax.nn.sigmoid(second_pre)).astype(jnp.bfloat16)
    second_delta = (local_cot.astype(jnp.float32) * silu_slope(second_pre)).astype(jnp.bfloat16)
    grad_second = weight_gradient(padded_act, second_delta)
    first_back = convolve(delta_pad(second_delta), flipped(second_weight), EDGE)
    first_delta = (first_back * silu_slope(first_pre)).astype(jnp.bfloat16)
    grad_first = weight_gradient(padded_input, first_delta)
    input_back = convolve(delta_pad(first_delta), flipped(first_weight), EDGE)
    grad_input = input_back.astype(jnp.bfloat16)
    grad_first, grad_second = lax.psum((grad_first, grad_second), ("scene", "brick"))
    grad_scale = float(lax.axis_size("scene") * lax.axis_size("brick") * VOX) ** (-0.5)
    return (output[None], grad_input[None], grad_first * grad_scale, grad_second * grad_scale)


def solution(mesh):
    in_specs = (
        P("scene", "brick", None),
        P("scene", "brick", None),
        P(),
        P(),
        P("scene", "brick"),
        P("scene", "brick"),
    )
    out_specs = (P("scene", "brick", None), P("scene", "brick", None), P(), P())
    return jax.shard_map(shards, mesh=mesh, in_specs=in_specs, out_specs=out_specs, check_vma=False)
```

profile of v0, /device:TPU:1, one launch (start us, length us, event | category | flops | bytes accessed | tf_op | source)
XLA Modules:
  0.0 597.6 jit_solution(4098987900195684948)
XLA Ops:
  7.9 1.0 copy.21
  9.8 4.8 collective-permute-start
  14.6 1.3 collective-permute-start.1
  17.0 1.0 fusion.27
  19.9 3.3 gather_fusion.1
  27.1 0.9 multiply_convert_fusion.1
  28.1 0.8 gather_fusion.2
  29.7 4.3 collective-permute-start.2
  34.0 1.3 collective-permute-start.3
  48.3 3.3 gather_fusion.3
  53.5 1.0 convolution_add_fusion.22
  54.7 1.0 convolution_add_fusion.21
  55.8 1.0 convolution_add_fusion.20
  56.9 1.0 convolution_add_fusion.19
  58.1 1.0 convolution_add_fusion.18
  59.2 1.0 convolution_add_fusion.17
  61.1 0.9 fusion.4
  63.6 0.8 gather_fusion.4
  65.1 5.5 collective-permute-start.4
  70.6 1.5 collective-permute-start.5
  72.3 0.9 concatenate.201
  73.2 3.1 collective-permute-done.5
  76.6 3.3 gather_fusion.5
  92.0 0.8 gather_fusion.6
  93.0 4.4 collective-permute-start.6
  97.4 1.3 collective-permute-start.7
  98.8 0.9 concatenate.200
  99.8 3.3 collective-permute-done.7
  103.3 3.3 gather_fusion.7
  115.6 0.8 fusion.3
  116.4 471.7 %all-reduce.7.cloned.1.call-done = (f32[1728,64]{0,1:T(8,128)}, f32[1728,64]{0,1:T(8,128)}) async-done(((f32[1728,64]{0,1:T(8,128)}, f32[1728,64]{0,1:T(8,128)}), (f32[1728,64]{0,1:T(8,128)}, f32[1728,64]{0,1:T(8,128)})) %all-reduce.7.cloned.1.call-update) | async-done | bytes 884752 | tf_op jit(solution)/shard_map/psum | solution.py:115
  588.1 1.9 broadcast_multiply_fusion
  (246 shorter events, 50.2 us)
Async XLA Ops:
  7.2 580.9 %all-reduce.7.cloned.1.call-start = ((), (), s32[]{:S(2)}) async-start(), calls=%async_computation | async-start | bytes 1835008 | tf_op jit(solution)/shard_map/psum | solution.py:115
  7.9 1.8 copy-start.38
  7.9 1.0 copy-start.37
  9.0 7.0 %copy-start.1 = (bf16[1728,64]{0,1:T(8,128)(2,1)S(1)}, bf16[1728,64]{0,1:T(8,128)(2,1)}, u32[]{:S(2)}) copy-start(bf16[1728,64]{0,1:T(8,128)(2,1)} %param.13) | copy-start | bytes 663556
  9.8 6.1 %copy-start.36 = (s32[1,1000]{1,0:T(1,128)S(1)}, s32[1,1000]{1,0:T(1,128)}, u32[]{:S(2)}) copy-start(s32[1,1000]{1,0:T(1,128)} %param.15) | copy-start | bytes 12004
  9.8 9.3 %collective-permute-start = (bf16[64,64]{1,0:T(8,128)(2,1)S(1)}, bf16[64,64]{1,0:T(8,128)(2,1)S(1)}, u32[]{:S(2)}, u32[]{:S(2)}) collective-permute-start(bf16[64,64]{1,0:T(8,128)(2,1)S(1)} %get-tuple-element.136), channel_id=1, source_target_pairs={{0,1},{1,2},{2,3},{3,4},{4,5},{5,6},{6,7},{7,8},{8,9},{9,10},{10,1... | collective-permute-start | bytes 24584 | tf_op jit(solution)/shard_map/ppermute | solution.py:15
  14.6 5.1 collective-permute-start.1
  16.0 7.3 %copy-start.34 = (pred[1000]{0:T(1024)(128)(4,1)}, pred[1000]{0:T(1024)(128)(4,1)S(1)}, u32[]{:S(2)}) copy-start(pred[1000]{0:T(1024)(128)(4,1)S(1)} %compare_and_fusion) | copy-start | bytes 3004
  17.0 1.0 copy-start
  18.0 1.9 copy-start.29
  19.1 0.8 copy-start.31
  27.0 0.9 copy-start.2
  29.7 17.8 %collective-permute-start.2 = (bf16[64,64]{0,1:T(8,128)(2,1)S(1)}, bf16[64,64]{0,1:T(8,128)(2,1)S(1)}, u32[]{:S(2)}, u32[]{:S(2)}) collective-permute-start(bf16[64,64]{0,1:T(8,128)(2,1)S(1)} %get-tuple-element.142), channel_id=1, source_target_pairs={{0,1},{1,2},{2,3},{3,4},{4,5},{5,6},{6,7},{7,8},{8,9},{9,10},{10,1... | collective-permute-start | bytes 24584 | tf_op jit(solution)/shard_map/ppermute | solution.py:15
  34.0 13.5 %collective-permute-start.3 = (bf16[64,64]{0,1:T(8,128)(2,1)S(1)}, bf16[64,64]{0,1:T(8,128)(2,1)S(1)}, u32[]{:S(2)}, u32[]{:S(2)}) collective-permute-start(bf16[64,64]{0,1:T(8,128)(2,1)S(1)} %get-tuple-element.143), channel_id=1, source_target_pairs={{1,0},{2,1},{3,2},{4,3},{5,4},{6,5},{7,6},{8,7},{9,8},{10,9},{11,1... | collective-permute-start | bytes 24584 | tf_op jit(solution)/shard_map/ppermute | solution.py:18
  35.3 0.8 copy-start.12
  35.6 1.2 copy-start.11
  36.8 0.9 copy-start.10
  37.4 0.9 copy-start.9
  38.2 0.9 copy-start.8
  38.9 0.9 copy-start.7
  39.7 0.9 copy-start.6
  40.4 0.9 copy-start.5
  48.3 3.3 copy-start.35
  60.2 0.8 copy-start.41
  65.1 8.0 %collective-permute-start.4 = (bf16[64,64]{0,1:T(8,128)(2,1)S(1)}, bf16[64,64]{0,1:T(8,128)(2,1)S(1)}, u32[]{:S(2)}, u32[]{:S(2)}) collective-permute-start(bf16[64,64]{0,1:T(8,128)(2,1)S(1)} %get-tuple-element.140), channel_id=1, source_target_pairs={{0,1},{1,2},{2,3},{3,4},{4,5},{5,6},{6,7},{7,8},{8,9},{9,10},{10,1... | collective-permute-start | bytes 24584 | tf_op jit(solution)/shard_map/ppermute | solution.py:15
  70.6 5.7 collective-permute-start.5
  80.9 0.8 copy-start.27
  88.5 0.9 copy-start.43
  89.5 0.9 copy-start.3
  93.0 6.8 %collective-permute-start.6 = (bf16[64,64]{0,1:T(8,128)(2,1)S(1)}, bf16[64,64]{0,1:T(8,128)(2,1)S(1)}, u32[]{:S(2)}, u32[]{:S(2)}) collective-permute-start(bf16[64,64]{0,1:T(8,128)(2,1)S(1)} %get-tuple-element.138), channel_id=1, source_target_pairs={{0,1},{1,2},{2,3},{3,4},{4,5},{5,6},{6,7},{7,8},{8,9},{9,10},{10,1... | collective-permute-start | bytes 24584 | tf_op jit(solution)/shard_map/ppermute | solution.py:15
  97.4 5.7 collective-permute-start.7
  588.1 1.9 copy-start.4
  (21 other events, 16.2 us)
Sparse Core Ops, SparseCore 0:
  99.9 488.1 all-reduce.6
where the time goes:
time: 600 us; the launch traced here: 598 us
  waiting for transfers between devices  479 us (80%)
  local copies, waits for them, and re-layouts  52.4 us (9%)
  starting transfers between devices  24.4 us (4%)
  matrix products  17.2 us (3%)
  between operations  15 us (2%)
  other arithmetic  9.86 us (2%)
    psum x1, waiting for transfers between devices, shards(): lax.psum((grad_first, grad_second), ('scene', 'brick'))  472 us
    ppermute x4, starting transfers between devices, extended(): lax.ppermute(lax.slice_in_dim(block, block.shape[dim] - width, None, axis...  19 us
    unnamed x92, local copies, waits for them, and re-layouts  16.1 us
    dot_general x36, matrix products, convolve(): jnp.dot(window_rows(padded, row_off, col_off, extent), weight[start:start...  14.1 us
    gather x4, local copies, waits for them, and re-layouts, assemble(): jnp.take(pool, gather_list, axis=0)  13.3 us
  transfers between devices with their start and end apart: 9, of which 4 were waited for; matrix products, arithmetic and copies ran while one was open for 4% of the time, Pallas kernels for 0%

commit v1 on v0

--- a/solution.py
+++ b/solution.py
@@ -1,10 +1,19 @@
+import functools
+
 import jax
 import jax.numpy as jnp
 from jax import lax
+from jax.experimental import pallas as pl
+from jax.experimental.pallas import tpu as pltpu
 from jax.sharding import PartitionSpec as P
 
 EDGE = 8
 VOX = 512
+C = 64
+TAPS = 27
+LANES = 128
+MESH = pl.DeviceIdType.MESH
+BLOCKS = 14
 
 
 def extended(block, sides, width):
@@ -68,13 +77,15 @@
         for col_off in range(3):
             pieces.append(
                 lax.dot_general(
+                    delta_rows,
                     window_rows(padded, row_off, col_off, EDGE),
-                    delta_rows,
                     (((0,), (0,)), ((), ())),
                     preferred_element_type=jnp.float32,
                 )
             )
-    return jnp.concatenate(pieces, axis=0)
+    wide = jnp.concatenate(pieces, axis=1)
+    wide = jnp.pad(wide, ((0, 0), (0, BLOCKS * LANES - wide.shape[1])))
+    return jnp.concatenate(jnp.split(wide, BLOCKS, axis=1), axis=0)
 
 
 def flipped(weight):
@@ -82,6 +93,204 @@
     return jnp.transpose(weight.reshape(27, width, width)[::-1], (0, 2, 1)).reshape(
         27 * width, width
     )
+
+
+def brick_grid(count):
+    for rows in (8, 4, 2):
+        if count % rows == 0 and count // rows > 1:
+            return rows, count // rows
+    return 1, count
+
+
+class Position:
+    def __init__(self, scenes, bricks):
+        self.scenes = scenes
+        self.bricks = bricks
+        self.rows, self.cols = brick_grid(bricks)
+        self.scene = lax.axis_index("scene")
+        self.brick = lax.axis_index("brick")
+        self.row = self.brick // self.cols
+        self.col = lax.rem(self.brick, self.cols)
+
+    def scene_peer(self, step):
+        return lax.rem(self.scene + step, self.scenes)
+
+    def row_peer(self, step):
+        return lax.rem(self.row + step, self.rows)
+
+    def col_peer(self, step):
+        return lax.rem(self.col + step, self.cols)
+
+    def scene_id(self, step):
+        return (self.scene_peer(step), self.brick)
+
+    def row_id(self, step):
+        return (self.scene, self.row_peer(step) * self.cols + self.col)
+
+    def col_id(self, step):
+        return (self.scene, self.row * self.cols + self.col_peer(step))
+
+    def reduce_peers(self):
+        peers = [self.scene_id(k) for k in range(1, self.scenes)]
+        peers += [self.row_id(k) for k in range(1, self.rows)]
+        peers += [self.col_id(k) for k in range(1, self.cols)]
+        return peers
+
+
+def meet(peers):
+    barrier = pltpu.get_barrier_semaphore()
+    for peer in peers:
+        pl.semaphore_signal(barrier, inc=1, device_id=peer, device_id_type=MESH)
+    pl.semaphore_wait(barrier, len(peers))
+
+
+def remote(src, dst, send_sem, recv_sem, peer):
+    copy = pltpu.make_async_remote_copy(
+        src_ref=src, dst_ref=dst, send_sem=send_sem, recv_sem=recv_sem,
+        device_id=peer, device_id_type=MESH,
+    )
+    copy.start()
+    return copy
+
+
+class Reduction:
+    def __init__(self, pos, refs):
+        self.pos = pos
+        (self.send_scene, self.recv_scene, self.send_row, self.recv_row,
+         self.slots, self.full, *sems) = refs
+        self.sems = [(sems[2 * i], sems[2 * i + 1]) for i in range(5)]
+        self.started = []
+
+    @staticmethod
+    def scratch(scenes, rows, cols):
+        piece = 1024 // scenes
+        small = piece // rows
+        counts = (scenes, rows, cols, rows, scenes)
+        sems = []
+        for count in counts:
+            sems += [pltpu.SemaphoreType.DMA((count - 1,))] * 2
+        return [
+            pltpu.VMEM((scenes, piece, LANES), jnp.bfloat16),
+            pltpu.VMEM((scenes - 1, piece, LANES), jnp.bfloat16),
+            pltpu.VMEM((rows, small, LANES), jnp.bfloat16),
+            pltpu.VMEM((rows - 1, small, LANES), jnp.bfloat16),
+            pltpu.VMEM((cols, small, LANES), jnp.bfloat16),
+            pltpu.VMEM((scenes, rows, small, LANES), jnp.bfloat16),
+        ] + sems
+
+    def put(self, block, values):
+        piece = self.send_scene.shape[1]
+        rows = values.shape[0]
+        start = block * rows
+        for at in range(start, start + rows, min(rows, piece)):
+            count = min(rows, piece)
+            self.send_scene[at // piece, pl.ds(at % piece, count), :] = values[
+                at - start : at - start + count
+            ]
+
+    def send(self, which, src, dst, peers):
+        self.current = []
+        for k, (peer, s, d) in enumerate(zip(peers, src, dst)):
+            sems = self.sems[which]
+            self.current.append(remote(s, d, sems[0].at[k], sems[1].at[k], peer))
+        self.started += self.current
+
+    def arrive(self):
+        for copy in self.current:
+            copy.wait_recv()
+
+    def start_scene(self):
+        pos = self.pos
+        n = pos.scenes
+        self.send(0, [self.send_scene.at[pos.scene_peer(k)] for k in range(1, n)],
+                  [self.recv_scene.at[k - 1] for k in range(1, n)],
+                  [pos.scene_id(k) for k in range(1, n)])
+
+    def start_row(self):
+        self.arrive()
+        pos = self.pos
+        n = pos.rows
+        total = self.send_scene[pos.scene].astype(jnp.float32)
+        for k in range(pos.scenes - 1):
+            total = total + self.recv_scene[k].astype(jnp.float32)
+        self.send_row[...] = total.astype(jnp.bfloat16).reshape(self.send_row.shape)
+        self.send(1, [self.send_row.at[pos.row_peer(k)] for k in range(1, n)],
+                  [self.recv_row.at[k - 1] for k in range(1, n)],
+                  [pos.row_id(k) for k in range(1, n)])
+
+    def start_col(self):
+        self.arrive()
+        pos = self.pos
+        n = pos.cols
+        total = self.send_row[pos.row].astype(jnp.float32)
+        for k in range(pos.rows - 1):
+            total = total + self.recv_row[k].astype(jnp.float32)
+        self.slots[pos.col] = total.astype(jnp.bfloat16)
+        own = self.slots.at[pos.col]
+        self.send(2, [own] * (n - 1), [own] * (n - 1), [pos.col_id(k) for k in range(1, n)])
+
+    def start_row_back(self):
+        self.arrive()
+        pos = self.pos
+        n = pos.rows
+        total = self.slots[0].astype(jnp.float32)
+        for k in range(1, pos.cols):
+            total = total + self.slots[k].astype(jnp.float32)
+        self.full[pos.scene, pos.row] = total.astype(jnp.bfloat16)
+        own = self.full.at[pos.scene, pos.row]
+        self.send(3, [own] * (n - 1), [own] * (n - 1), [pos.row_id(k) for k in range(1, n)])
+
+    def start_scene_back(self):
+        self.arrive()
+        pos = self.pos
+        n = pos.scenes
+        own = self.full.at[pos.scene]
+        self.send(4, [own] * (n - 1), [own] * (n - 1), [pos.scene_id(k) for k in range(1, n)])
+
+    def finish(self, out, scale):
+        self.arrive()
+        everything = self.full[...].reshape(1024, LANES)
+        for block in range(BLOCKS):
+            rows = min(LANES, TAPS * C - block * LANES)
+            piece = everything[block * C : (block + 1) * C].astype(jnp.float32) * scale
+            out[pl.ds(block * LANES, rows), :] = jnp.transpose(piece)[:rows]
+        for copy in self.started:
+            copy.wait_send()
+
+
+def reduce_kernel(scenes, bricks, first, second, out_first, out_second, *scratch):
+    pos = Position(scenes, bricks)
+    meet(pos.reduce_peers())
+    half = len(scratch) // 2
+    sums = [Reduction(pos, scratch[:half]), Reduction(pos, scratch[half:])]
+    scale = float(scenes * bricks * VOX) ** (-0.5)
+    for one, source in zip(sums, (first, second)):
+        for block in range(BLOCKS):
+            one.put(block, source[pl.ds(block * C, C), :].astype(jnp.bfloat16))
+        for block in (BLOCKS, BLOCKS + 1):
+            one.put(block, jnp.zeros((C, LANES), jnp.bfloat16))
+        one.start_scene()
+    for step in ("start_row", "start_col", "start_row_back", "start_scene_back"):
+        for one in sums:
+            getattr(one, step)()
+    for one, out in zip(sums, (out_first, out_second)):
+        one.finish(out, scale)
+
+
+def reduce_all(first, second):
+    scenes, bricks = lax.axis_size("scene"), lax.axis_size("brick")
+    rows, cols = brick_grid(bricks)
+    shape = jax.ShapeDtypeStruct((TAPS * C, C), jnp.float32)
+    return pl.pallas_call(
+        functools.partial(reduce_kernel, scenes, bricks),
+        out_shape=(shape, shape),
+        in_specs=[pl.BlockSpec(memory_space=pltpu.VMEM)] * 2,
+        out_specs=[pl.BlockSpec(memory_space=pltpu.VMEM)] * 2,
+        scratch_shapes=Reduction.scratch(scenes, rows, cols) * 2,
+        compiler_params=pltpu.CompilerParams(
+            collective_id=0, has_side_effects=True, vmem_limit_bytes=48 * 1024 * 1024
+        ),
+    )(first, second)
 
 
 def shards(features, cotangent, first_weight, second_weight, send_rows, gather_rows):
@@ -92,10 +301,6 @@
     slot_width = send_list.shape[0] // 2
 
     def forward_pad(values):
-        arrived = extended(outgoing_rows(values, send_list), (("brick", 0),), slot_width)
-        return assemble(values, arrived, gather_list, slot_width)
-
-    def delta_pad(values):
         arrived = extended(outgoing_rows(values, send_list), (("brick", 0),), slot_width)
         return assemble(values, arrived, gather_list, slot_width)
 
@@ -107,14 +312,13 @@
     output = (second_pre * jax.nn.sigmoid(second_pre)).astype(jnp.bfloat16)
     second_delta = (local_cot.astype(jnp.float32) * silu_slope(second_pre)).astype(jnp.bfloat16)
     grad_second = weight_gradient(padded_act, second_delta)
-    first_back = convolve(delta_pad(second_delta), flipped(second_weight), EDGE)
+    first_back = convolve(forward_pad(second_delta), flipped(second_weight), EDGE)
     first_delta = (first_back * silu_slope(first_pre)).astype(jnp.bfloat16)
     grad_first = weight_gradient(padded_input, first_delta)
-    input_back = convolve(delta_pad(first_delta), flipped(first_weight), EDGE)
+    input_back = convolve(forward_pad(first_delta), flipped(first_weight), EDGE)
     grad_input = input_back.astype(jnp.bfloat16)
-    grad_first, grad_second = lax.psum((grad_first, grad_second), ("scene", "brick"))
-    grad_scale = float(lax.axis_size("scene") * lax.axis_size("brick") * VOX) ** (-0.5)
-    return (output[None], grad_input[None], grad_first * grad_scale, grad_second * grad_scale)
+    grad_first, grad_second = reduce_all(grad_first, grad_second)
+    return (output[None], grad_input[None], grad_first, grad_second)
 
 
 def solution(mesh):

time: 600 us -> 173 us (0.29)
  waiting for transfers between devices: 479 us -> 4.87 us
  Pallas kernels: 0 us -> 53.4 us
  between operations: 15 us -> 1.62 us
  local copies, waits for them, and re-layouts: 52.4 us -> 58.9 us
    psum x1 -> x0, waiting for transfers between devices: 472 us -> none  [shards(): lax.psum((grad_first, grad_second), ('scene', 'brick'))]
    pallas_call x0 -> x1, Pallas kernels: none -> 53.4 us  [reduce_all(): pl.pallas_call(functools.partial(reduce_kernel, scenes, bricks), out_shap...]
    unnamed x92 -> x118, local copies, waits for them, and re-layouts: 16.1 us -> 23.8 us
  transfers between devices with their start and end apart: 9 -> 8, of which waited for: 4 -> 2; matrix products, arithmetic and copies ran while one was open for 4% -> 10% of each run, Pallas kernels for 0% -> 31%
where the time goes in v1:
time: 173 us; the launch traced here: 171 us
  local copies, waits for them, and re-layouts  58.9 us (34%)
  Pallas kernels  53.4 us (31%)
  starting transfers between devices  24 us (14%)
  matrix products  20.3 us (12%)
  other arithmetic  7.82 us (5%)
  waiting for transfers between devices  4.87 us (3%)
    pallas_call x1, Pallas kernels, reduce_all(): pl.pallas_call(functools.partial(reduce_kernel, scenes, bricks), out_shap...  53.4 us
    unnamed x118, local copies, waits for them, and re-layouts  23.8 us
    ppermute x4, starting transfers between devices, extended(): lax.ppermute(lax.slice_in_dim(block, block.shape[dim] - width, None, axis...  18.6 us
    dot_general x36, matrix products, convolve(): jnp.dot(window_rows(padded, row_off, col_off, extent), weight[start:start...  14 us
    gather x4, local copies, waits for them, and re-layouts, assemble(): jnp.take(pool, gather_list, axis=0)  13.3 us
    slice x20, local copies, waits for them, and re-layouts, convolve(): weight[start:start + 3 * width]  12.5 us
    dot_general x18, matrix products, weight_gradient(): lax.dot_general(delta_rows, window_rows(padded, row_off, col_off, EDGE),...  6.26 us
    ppermute x4, starting transfers between devices, extended(): lax.ppermute(lax.slice_in_dim(block, 0, width, axis=dim), axis, backward)  5.35 us
  transfers between devices with their start and end apart: 8, of which 2 were waited for; matrix products, arithmetic and copies ran while one was open for 10% of the time, Pallas kernels for 31%

profile of v1, /device:TPU:1, one launch (start us, length us, event | category | flops | bytes accessed | tf_op | source)
XLA Modules:
  0.0 170.9 jit_solution(16707793653738718245)
XLA Ops:
  1.4 1.0 copy.23
  3.2 4.8 %collective-permute-start = (bf16[64,64]{1,0:T(8,128)(2,1)S(1)}, bf16[64,64]{1,0:T(8,128)(2,1)S(1)}, u32[]{:S(2)}, u32[]{:S(2)}) collective-permute-start(bf16[64,64]{1,0:T(8,128)(2,1)S(1)} %get-tuple-element.146), channel_id=1, source_target_pairs={{0,1},{1,2},{2,3},{3,4},{4,5},{5,6},{6,7},{7,8},{8,9},{9,10},{10,1... | collective-permute-start | bytes 24584 | tf_op jit(solution)/shard_map/ppermute | solution.py:24
  8.1 1.3 collective-permute-start.1
  10.5 1.0 fusion.27
  13.4 3.3 %gather_fusion.1 = bf16[1000,64]{1,0:T(8,128)(2,1)S(1)} fusion(bf16[641,64]{1,0:T(8,128)(2,1)S(1)} %maximum_maximum_fusion, s32[1024]{0:T(1024)S(1)} %pad_clamp_fusion), kind=kCustom, calls=%fused_computation.1.clone | custom fusion | bytes 260000 | tf_op jit(solution)/shard_map/jit(_take)/gather | solution.py:47
  21.1 0.9 multiply_convert_fusion.1
  23.5 4.0 %collective-permute-start.2 = (bf16[64,64]{0,1:T(8,128)(2,1)S(1)}, bf16[64,64]{0,1:T(8,128)(2,1)S(1)}, u32[]{:S(2)}, u32[]{:S(2)}) collective-permute-start(bf16[64,64]{0,1:T(8,128)(2,1)S(1)} %get-tuple-element.152), channel_id=1, source_target_pairs={{0,1},{1,2},{2,3},{3,4},{4,5},{5,6},{6,7},{7,8},{8,9},{9,10},{10,1... | collective-permute-start | bytes 24584 | tf_op jit(solution)/shard_map/ppermute | solution.py:24
  27.5 1.3 collective-permute-start.3
  42.0 3.3 %gather_fusion.3 = bf16[1000,64]{1,0:T(8,128)(2,1)S(1)} fusion(bf16[641,64]{1,0:T(8,128)(2,1)S(1)} %copy.27, s32[1024]{0:T(1024)S(1)} %pad_clamp_fusion), kind=kCustom, calls=%fused_computation.5.clone | custom fusion | bytes 260000 | tf_op jit(solution)/shard_map/jit(_take)/gather | solution.py:47
  47.2 1.0 convolution_add_fusion.22
  48.3 1.0 convolution_add_fusion.21
  49.5 1.0 convolution_add_fusion.20
  50.6 1.0 convolution_add_fusion.19
  51.8 1.0 convolution_add_fusion.18
  52.9 1.0 convolution_add_fusion.17
  54.7 0.9 fusion.4
  55.6 0.8 fusion.61
  56.6 0.8 fusion.59
  57.4 0.8 fusion.58
  58.2 0.8 fusion.57
  65.0 5.8 %collective-permute-start.4 = (bf16[64,64]{0,1:T(8,128)(2,1)S(1)}, bf16[64,64]{0,1:T(8,128)(2,1)S(1)}, u32[]{:S(2)}, u32[]{:S(2)}) collective-permute-start(bf16[64,64]{0,1:T(8,128)(2,1)S(1)} %get-tuple-element.150), channel_id=1, source_target_pairs={{0,1},{1,2},{2,3},{3,4},{4,5},{5,6},{6,7},{7,8},{8,9},{9,10},{10,1... | collective-permute-start | bytes 24584 | tf_op jit(solution)/shard_map/ppermute | solution.py:24
  70.9 1.5 collective-permute-start.5
  72.4 4.2 %collective-permute-done.5 = bf16[64,64]{0,1:T(8,128)(2,1)S(1)} collective-permute-done((bf16[64,64]{0,1:T(8,128)(2,1)S(1)}, bf16[64,64]{0,1:T(8,128)(2,1)S(1)}, u32[]{:S(2)}, u32[]{:S(2)}) %collective-permute-start.5) | collective-permute-done | bytes 8224 | tf_op jit(solution)/shard_map/ppermute | solution.py:27
  76.8 3.3 %gather_fusion.5 = bf16[1000,64]{1,0:T(8,128)(2,1)S(1)} fusion(bf16[641,64]{1,0:T(8,128)(2,1)S(1)} %copy.30, s32[1024]{0:T(1024)S(1)} %pad_clamp_fusion), kind=kCustom, calls=%fused_computation.6.clone | custom fusion | bytes 260000 | tf_op jit(solution)/shard_map/jit(_take)/gather | solution.py:47
  90.7 0.8 fusion.52
  96.1 4.0 %collective-permute-start.6 = (bf16[64,64]{0,1:T(8,128)(2,1)S(1)}, bf16[64,64]{0,1:T(8,128)(2,1)S(1)}, u32[]{:S(2)}, u32[]{:S(2)}) collective-permute-start(bf16[64,64]{0,1:T(8,128)(2,1)S(1)} %get-tuple-element.148), channel_id=1, source_target_pairs={{0,1},{1,2},{2,3},{3,4},{4,5},{5,6},{6,7},{7,8},{8,9},{9,10},{10,1... | collective-permute-start | bytes 24584 | tf_op jit(solution)/shard_map/ppermute | solution.py:24
  100.1 1.3 collective-permute-start.7
  101.4 53.4 %shard_map.93 = (f32[1728,64]{1,0:T(8,128)S(1)}, f32[1728,64]{1,0:T(8,128)S(1)}) custom-call(f32[896,128]{1,0:T(8,128)S(1)} %constant_dynamic-update-slice_fusion.first, f32[896,128]{1,0:T(8,128)S(1)} %constant_dynamic-update-slice_fusion.14.second), custom_call_target="tpu_custom_call" | custom-call | tf_op jit(solution)/shard_map/pallas_call | solution.py:284
  154.9 1.1 copy.52
  155.9 1.1 copy.53
  157.2 3.3 %gather_fusion.7 = bf16[1000,64]{1,0:T(8,128)(2,1)S(1)} fusion(bf16[641,64]{1,0:T(8,128)(2,1)S(1)} %copy.42, s32[1024]{0:T(1024)S(1)} %pad_clamp_fusion), kind=kCustom, calls=%fused_computation.7.clone | custom fusion | bytes 260000 | tf_op jit(solution)/shard_map/jit(_take)/gather | solution.py:47
  170.1 0.8 fusion.3
  (278 shorter events, 57.8 us)
Async XLA Ops:
  1.4 1.8 %copy-start.40 = (pred[128]{0:T(512)(128)(4,1)}, pred[128]{0:T(512)(128)(4,1)S(1)}, u32[]{:S(2)}) copy-start(pred[128]{0:T(512)(128)(4,1)S(1)} %compare_and_fusion.1) | copy-start | bytes 388
  2.4 7.0 %copy-start.3 = (bf16[1728,64]{0,1:T(8,128)(2,1)S(1)}, bf16[1728,64]{0,1:T(8,128)(2,1)}, u32[]{:S(2)}) copy-start(bf16[1728,64]{0,1:T(8,128)(2,1)} %param.13) | copy-start | bytes 663556
  3.2 6.1 %copy-start.39 = (s32[1,1000]{1,0:T(1,128)S(1)}, s32[1,1000]{1,0:T(1,128)}, u32[]{:S(2)}) copy-start(s32[1,1000]{1,0:T(1,128)} %param.15) | copy-start | bytes 12004
  3.2 9.3 %collective-permute-start = (bf16[64,64]{1,0:T(8,128)(2,1)S(1)}, bf16[64,64]{1,0:T(8,128)(2,1)S(1)}, u32[]{:S(2)}, u32[]{:S(2)}) collective-permute-start(bf16[64,64]{1,0:T(8,128)(2,1)S(1)} %get-tuple-element.146), channel_id=1, source_target_pairs={{0,1},{1,2},{2,3},{3,4},{4,5},{5,6},{6,7},{7,8},{8,9},{9,10},{10,1... | collective-permute-start | bytes 24584 | tf_op jit(solution)/shard_map/ppermute | solution.py:24
  8.1 5.1 %collective-permute-start.1 = (bf16[64,64]{1,0:T(8,128)(2,1)S(1)}, bf16[64,64]{1,0:T(8,128)(2,1)S(1)}, u32[]{:S(2)}, u32[]{:S(2)}) collective-permute-start(bf16[64,64]{1,0:T(8,128)(2,1)S(1)} %get-tuple-element.147), channel_id=1, source_target_pairs={{1,0},{2,1},{3,2},{4,3},{5,4},{6,5},{7,6},{8,7},{9,8},{10,9},{11,1... | collective-permute-start | bytes 24584 | tf_op jit(solution)/shard_map/ppermute | solution.py:27
  10.5 1.0 copy-start.2
  21.0 0.9 copy-start.4
  23.5 18.3 %collective-permute-start.2 = (bf16[64,64]{0,1:T(8,128)(2,1)S(1)}, bf16[64,64]{0,1:T(8,128)(2,1)S(1)}, u32[]{:S(2)}, u32[]{:S(2)}) collective-permute-start(bf16[64,64]{0,1:T(8,128)(2,1)S(1)} %get-tuple-element.152), channel_id=1, source_target_pairs={{0,1},{1,2},{2,3},{3,4},{4,5},{5,6},{6,7},{7,8},{8,9},{9,10},{10,1... | collective-permute-start | bytes 24584 | tf_op jit(solution)/shard_map/ppermute | solution.py:24
  27.5 14.3 %collective-permute-start.3 = (bf16[64,64]{0,1:T(8,128)(2,1)S(1)}, bf16[64,64]{0,1:T(8,128)(2,1)S(1)}, u32[]{:S(2)}, u32[]{:S(2)}) collective-permute-start(bf16[64,64]{0,1:T(8,128)(2,1)S(1)} %get-tuple-element.153), channel_id=1, source_target_pairs={{1,0},{2,1},{3,2},{4,3},{5,4},{6,5},{7,6},{8,7},{9,8},{10,9},{11,1... | collective-permute-start | bytes 24584 | tf_op jit(solution)/shard_map/ppermute | solution.py:27
  28.8 0.8 copy-start.20
  29.1 1.2 copy-start.19
  30.2 0.9 copy-start.18
  30.9 0.9 copy-start.17
  31.7 0.9 copy-start.16
  32.3 0.8 copy-start.15
  33.2 0.9 copy-start.14
  33.8 0.9 copy-start.13
  34.7 0.9 copy-start.12
  53.9 0.8 copy-start.44
  60.6 0.8 copy-start.8
  60.7 0.9 copy-start.7
  61.6 0.8 copy-start.6
  61.6 0.9 copy-start.10
  62.7 0.9 copy-start.9
  65.0 7.3 %collective-permute-start.4 = (bf16[64,64]{0,1:T(8,128)(2,1)S(1)}, bf16[64,64]{0,1:T(8,128)(2,1)S(1)}, u32[]{:S(2)}, u32[]{:S(2)}) collective-permute-start(bf16[64,64]{0,1:T(8,128)(2,1)S(1)} %get-tuple-element.150), channel_id=1, source_target_pairs={{0,1},{1,2},{2,3},{3,4},{4,5},{5,6},{6,7},{7,8},{8,9},{9,10},{10,1... | collective-permute-start | bytes 24584 | tf_op jit(solution)/shard_map/ppermute | solution.py:24
  70.9 5.7 %collective-permute-start.5 = (bf16[64,64]{0,1:T(8,128)(2,1)S(1)}, bf16[64,64]{0,1:T(8,128)(2,1)S(1)}, u32[]{:S(2)}, u32[]{:S(2)}) collective-permute-start(bf16[64,64]{0,1:T(8,128)(2,1)S(1)} %get-tuple-element.151), channel_id=1, source_target_pairs={{1,0},{2,1},{3,2},{4,3},{5,4},{6,5},{7,6},{8,7},{9,8},{10,9},{11,1... | collective-permute-start | bytes 24584 | tf_op jit(solution)/shard_map/ppermute | solution.py:27
  88.8 0.9 copy-start.46
  89.7 0.9 copy-start.5
  90.7 0.9 copy-start.1
  93.5 0.8 copy-start.11
  96.1 60.8 %collective-permute-start.6 = (bf16[64,64]{0,1:T(8,128)(2,1)S(1)}, bf16[64,64]{0,1:T(8,128)(2,1)S(1)}, u32[]{:S(2)}, u32[]{:S(2)}) collective-permute-start(bf16[64,64]{0,1:T(8,128)(2,1)S(1)} %get-tuple-element.148), channel_id=1, source_target_pairs={{0,1},{1,2},{2,3},{3,4},{4,5},{5,6},{6,7},{7,8},{8,9},{9,10},{10,1... | collective-permute-start | bytes 24584 | tf_op jit(solution)/shard_map/ppermute | solution.py:24
  100.1 56.9 %collective-permute-start.7 = (bf16[64,64]{0,1:T(8,128)(2,1)S(1)}, bf16[64,64]{0,1:T(8,128)(2,1)S(1)}, u32[]{:S(2)}, u32[]{:S(2)}) collective-permute-start(bf16[64,64]{0,1:T(8,128)(2,1)S(1)} %get-tuple-element.149), channel_id=1, source_target_pairs={{1,0},{2,1},{3,2},{4,3},{5,4},{6,5},{7,6},{8,7},{9,8},{10,9},{11,1... | collective-permute-start | bytes 24584 | tf_op jit(solution)/shard_map/ppermute | solution.py:27
  (23 other events, 17.6 us)

commit v2 on v1

v2 whole, which is shorter than its diff:
```python
import functools

import jax
import jax.numpy as jnp
from jax import lax
from jax.experimental import pallas as pl
from jax.experimental.pallas import tpu as pltpu
from jax.sharding import PartitionSpec as P

EDGE = 8
VOX = 512
C = 64
TAPS = 27
LANES = 128
MESH = pl.DeviceIdType.MESH
BLOCKS = 14
SPAN = EDGE + 2
CELLS = SPAN**3
SLAB = SPAN * SPAN * EDGE
POOL = VOX + LANES
PAIRS = 9
DEEP = 256
EXCHANGES = 4


def brick_grid(count):
    for rows in (8, 4, 2):
        if count % rows == 0 and count // rows > 1:
            return rows, count // rows
    return 1, count


class Position:
    def __init__(self, scenes, bricks):
        self.scenes = scenes
        self.bricks = bricks
        self.rows, self.cols = brick_grid(bricks)
        self.scene = lax.axis_index("scene")
        self.brick = lax.axis_index("brick")
        self.row = self.brick // self.cols
        self.col = lax.rem(self.brick, self.cols)

    def scene_peer(self, step):
        return lax.rem(self.scene + step, self.scenes)

    def row_peer(self, step):
        return lax.rem(self.row + step, self.rows)

    def col_peer(self, step):
        return lax.rem(self.col + step, self.cols)

    def scene_id(self, step):
        return (self.scene_peer(step), self.brick)

    def row_id(self, step):
        return (self.scene, self.row_peer(step) * self.cols + self.col)

    def col_id(self, step):
        return (self.scene, self.row * self.cols + self.col_peer(step))

    def down_id(self):
        return (self.scene, lax.rem(self.brick + self.bricks - 1, self.bricks))

    def up_id(self):
        return (self.scene, lax.rem(self.brick + 1, self.bricks))

    def reduce_peers(self):
        peers = [self.scene_id(k) for k in range(1, self.scenes)]
        peers += [self.row_id(k) for k in range(1, self.rows)]
        peers += [self.col_id(k) for k in range(1, self.cols)]
        return peers


def greet(peers):
    barrier = pltpu.get_barrier_semaphore()
    for peer in peers:
        pl.semaphore_signal(barrier, inc=1, device_id=peer, device_id_type=MESH)


def await_peers(peers):
    pl.semaphore_wait(pltpu.get_barrier_semaphore(), len(peers))


def remote(src, dst, send_sem, recv_sem, peer):
    copy = pltpu.make_async_remote_copy(
        src_ref=src, dst_ref=dst, send_sem=send_sem, recv_sem=recv_sem,
        device_id=peer, device_id_type=MESH,
    )
    copy.start()
    return copy


class Reduction:
    def __init__(self, pos, refs):
        self.pos = pos
        (self.send_scene, self.recv_scene, self.send_row, self.recv_row,
         self.slots, self.full, *sems) = refs
        self.sems = [(sems[2 * i], sems[2 * i + 1]) for i in range(5)]
        self.started = []

    @staticmethod
    def scratch(scenes, rows, cols):
        piece = 1024 // scenes
        small = piece // rows
        counts = (scenes, rows, cols, rows, scenes)
        sems = []
        for count in counts:
            sems += [pltpu.SemaphoreType.DMA((count - 1,))] * 2
        return [
            pltpu.VMEM((scenes, piece, LANES), jnp.bfloat16),
            pltpu.VMEM((scenes - 1, piece, LANES), jnp.bfloat16),
            pltpu.VMEM((rows, small, LANES), jnp.bfloat16),
            pltpu.VMEM((rows - 1, small, LANES), jnp.bfloat16),
            pltpu.VMEM((cols, small, LANES), jnp.bfloat16),
            pltpu.VMEM((scenes, rows, small, LANES), jnp.bfloat16),
        ] + sems

    def put(self, block, values):
        piece = self.send_scene.shape[1]
        rows = values.shape[0]
        start = block * rows
        for at in range(start, start + rows, min(rows, piece)):
            count = min(rows, piece)
            self.send_scene[at // piece, pl.ds(at % piece, count), :] = values[
                at - start : at - start + count
            ]

    def send(self, which, src, dst, peers):
        self.current = []
        for k, (peer, s, d) in enumerate(zip(peers, src, dst)):
            sems = self.sems[which]
            self.current.append(remote(s, d, sems[0].at[k], sems[1].at[k], peer))
        self.started += self.current

    def arrive(self):
        for copy in self.current:
            copy.wait_recv()

    def start_scene(self):
        pos = self.pos
        n = pos.scenes
        self.send(0, [self.send_scene.at[pos.scene_peer(k)] for k in range(1, n)],
                  [self.recv_scene.at[k - 1] for k in range(1, n)],
                  [pos.scene_id(k) for k in range(1, n)])

    def start_row(self):
        self.arrive()
        pos = self.pos
        n = pos.rows
        total = self.send_scene[pos.scene].astype(jnp.float32)
        for k in range(pos.scenes - 1):
            total = total + self.recv_scene[k].astype(jnp.float32)
        self.send_row[...] = total.astype(jnp.bfloat16).reshape(self.send_row.shape)
        self.send(1, [self.send_row.at[pos.row_peer(k)] for k in range(1, n)],
                  [self.recv_row.at[k - 1] for k in range(1, n)],
                  [pos.row_id(k) for k in range(1, n)])

    def start_col(self):
        self.arrive()
        pos = self.pos
        n = pos.cols
        total = self.send_row[pos.row].astype(jnp.float32)
        for k in range(pos.rows - 1):
            total = total + self.recv_row[k].astype(jnp.float32)
        self.slots[pos.col] = total.astype(jnp.bfloat16)
        own = self.slots.at[pos.col]
        self.send(2, [own] * (n - 1), [own] * (n - 1), [pos.col_id(k) for k in range(1, n)])

    def start_row_back(self):
        self.arrive()
        pos = self.pos
        n = pos.rows
        total = self.slots[0].astype(jnp.float32)
        for k in range(1, pos.cols):
            total = total + self.slots[k].astype(jnp.float32)
        self.full[pos.scene, pos.row] = total.astype(jnp.bfloat16)
        own = self.full.at[pos.scene, pos.row]
        self.send(3, [own] * (n - 1), [own] * (n - 1), [pos.row_id(k) for k in range(1, n)])

    def start_scene_back(self):
        self.arrive()
        pos = self.pos
        n = pos.scenes
        own = self.full.at[pos.scene]
        self.send(4, [own] * (n - 1), [own] * (n - 1), [pos.scene_id(k) for k in range(1, n)])

    def finish(self, out, scale):
        self.arrive()
        everything = self.full[...].reshape(1024, LANES)
        for block in range(BLOCKS):
            piece = everything[block * C : (block + 1) * C].astype(jnp.float32) * scale
            piece = jnp.transpose(piece)
            if block < PAIRS:
                out[pl.ds(block * 3 * C, 2 * C), :] = piece
            else:
                for half in range(2):
                    pair = 2 * (block - PAIRS) + half
                    if pair < PAIRS:
                        out[pl.ds(pair * 3 * C + 2 * C, C), :] = piece[half * C : (half + 1) * C]
        for copy in self.started:
            copy.wait_send()


def hot(columns, width):
    lane = lax.broadcasted_iota(jnp.int32, (1, LANES), 1).astype(jnp.float32)
    parts = [
        jnp.where(columns == lane + float(at), 1.0, 0.0).astype(jnp.bfloat16)
        for at in range(0, width, LANES)
    ]
    return jnp.concatenate(parts, axis=1)


def as_columns(row):
    return jnp.transpose(jnp.broadcast_to(row, (LANES, LANES)))


def twice(values):
    return jnp.concatenate([values, values], axis=1)


def matmul(left, right):
    return jnp.dot(left, right, preferred_element_type=jnp.float32)


class Field:
    def __init__(self, even, odd):
        self.even = even
        self.odd = odd

    def window(self, pair):
        a, b = pair // 3, pair % 3
        if b == 1:
            rows = self.odd[a : a + EDGE]
        else:
            rows = self.even[a : a + EDGE, EDGE * b : EDGE * b + VOX // EDGE]
        return rows.reshape(VOX, DEEP)

    def fill(self, pads):
        low = lax.broadcasted_iota(jnp.int32, (1, LANES), 1) < C
        first = jnp.where(low, pads[0][...], pads[1][...]).reshape(SPAN, SPAN * EDGE, LANES)
        last = pads[2][...].reshape(SPAN, SPAN * EDGE, LANES)
        odd = slice(EDGE, EDGE + VOX // EDGE)
        for at, part in ((0, first), (LANES, last)):
            self.even[:, :, at : at + LANES] = part.astype(jnp.bfloat16)
            self.odd[:, :, at : at + LANES] = part[:, odd].astype(jnp.bfloat16)

    def conv(self, weight):
        total = matmul(self.window(0), weight[0])
        for pair in range(1, PAIRS):
            total = total + matmul(self.window(pair), weight[pair])
        return total


def weight_gradient(field, delta, put):
    low = lax.broadcasted_iota(jnp.int32, (1, LANES), 1) < C
    turned = jnp.transpose(delta[:, :C]).astype(jnp.bfloat16)
    held = None
    for pair in range(PAIRS):
        got = matmul(turned, field.window(pair))
        put(pair, got[:, :LANES].astype(jnp.bfloat16))
        last = got[:, LANES:]
        if pair % 2 == 0:
            held = last
        else:
            put(PAIRS + pair // 2, jnp.where(low, held, last).astype(jnp.bfloat16))
    put(PAIRS + PAIRS // 2, held.astype(jnp.bfloat16))


def spread_weight(weight, plain, flip):
    zero = jnp.zeros((C, LANES), jnp.bfloat16)
    for pair in range(PAIRS):
        plain[pair, : 3 * C, :] = twice(weight[pl.ds(pair * 3 * C, 3 * C), :])
        plain[pair, 3 * C :, :] = zero
        flip[pair, 3 * C :, :] = zero
        for c in range(3):
            source = (TAPS - 1 - (3 * pair + c)) * C
            block = twice(weight[pl.ds(source, C), :].astype(jnp.float32))
            block = jnp.transpose(block)[:C]
            block = twice(block)
            flip[pair, c * C : (c + 1) * C, :] = block.astype(jnp.bfloat16)


def step_kernel(
    scenes, bricks, features, cotangent, first_weight, second_weight, send_rows, gather_rows,
    output, grad_input, grad_first, grad_second,
    indices, columns, gather_hot, send_hot, pads, halo_out, halo_in, halo_send, halo_recv,
    first_plain, first_flip, second_plain, second_flip,
    even_in, odd_in, even_act, odd_act, even_delta, odd_delta, first_pre_ref, *reduction,
):
    pos = Position(scenes, bricks)
    peers = [pos.down_id(), pos.up_id()] + pos.reduce_peers()
    greet(peers)
    half = len(reduction) // 2
    first_sum = Reduction(pos, reduction[:half])
    second_sum = Reduction(pos, reduction[half:])
    halos = []

    def send_halo(values):
        at = len(halos)
        halo_out[at] = matmul(send_hot[...], values).astype(jnp.bfloat16)
        if at == 0:
            await_peers(peers)
        halos.append([
            remote(halo_out.at[at, pl.ds(64 * way, 64)], halo_in.at[at, pl.ds(64 * (1 - way), 64)],
                   halo_send.at[at, way], halo_recv.at[at, way], peer)
            for way, peer in enumerate((pos.down_id(), pos.up_id()))
        ])

    def gather_local(values):
        for c in range(3):
            pads[c] = matmul(gather_hot[c, :, :VOX], values)

    def gather_halo(field):
        at = len(halos) - 1
        for copy in halos[at]:
            copy.wait_recv()
        rows = halo_in[at]
        for c in range(3):
            pads[c] = pads[c] + matmul(gather_hot[c, :, VOX:], rows)
        field.fill([pads.at[c] for c in range(3)])

    send_hot[...] = hot(as_columns(send_rows[...].astype(jnp.float32)), VOX)
    feature_rows = twice(features[...])
    send_halo(feature_rows)

    indices[...] = jnp.full(indices.shape, float(POOL), jnp.float32)
    indices[:, :CELLS] = jnp.broadcast_to(gather_rows[...].astype(jnp.float32), (EDGE, CELLS))
    for at in range(0, 1024, LANES):
        columns[pl.ds(at, LANES), :] = as_columns(indices[0:1, at : at + LANES])
    for c in range(3):
        taken = jnp.concatenate(
            [columns[pl.ds(SPAN * row + c, EDGE), :] for row in range(SPAN * SPAN)], axis=0
        )
        gather_hot[c] = hot(taken, POOL)
    gather_local(feature_rows)
    spread_weight(first_weight, first_plain, first_flip)
    spread_weight(second_weight, second_plain, second_flip)
    for one in (first_sum, second_sum):
        for block in (BLOCKS, BLOCKS + 1):
            one.put(block, jnp.zeros((C, LANES), jnp.bfloat16))

    field_in = Field(even_in, odd_in)
    field_act = Field(even_act, odd_act)
    field_delta = Field(even_delta, odd_delta)

    gather_halo(field_in)
    first_pre = field_in.conv(first_plain)
    first_pre_ref[...] = first_pre
    first_act = (first_pre * jax.nn.sigmoid(first_pre)).astype(jnp.bfloat16)
    send_halo(first_act)
    gather_local(first_act)
    gather_halo(field_act)
    second_pre = field_act.conv(second_plain)
    sig = jax.nn.sigmoid(second_pre)
    slope = sig * (1.0 + second_pre * (1.0 - sig))
    second_delta32 = twice(cotangent[...]).astype(jnp.float32) * slope
    second_delta = second_delta32.astype(jnp.bfloat16)
    send_halo(second_delta)
    output[...] = (second_pre * sig).astype(jnp.bfloat16)[:, :C]
    weight_gradient(field_act, second_delta32, second_sum.put)
    second_sum.start_scene()
    gather_local(second_delta)
    gather_halo(field_delta)
    first_back = field_delta.conv(second_flip)
    first_pre = first_pre_ref[...]
    sig = jax.nn.sigmoid(first_pre)
    slope = sig * (1.0 + first_pre * (1.0 - sig))
    first_delta32 = first_back * slope
    first_delta = first_delta32.astype(jnp.bfloat16)
    send_halo(first_delta)
    weight_gradient(field_in, first_delta32, first_sum.put)
    first_sum.start_scene()
    second_sum.start_row()
    gather_local(first_delta)
    gather_halo(field_delta)
    second_sum.start_col()
    first_sum.start_row()
    grad_input[...] = field_delta.conv(first_flip).astype(jnp.bfloat16)[:, :C]
    second_sum.start_row_back()
    first_sum.start_col()
    second_sum.start_scene_back()
    first_sum.start_row_back()
    first_sum.start_scene_back()
    scale = float(scenes * bricks * VOX) ** (-0.5)
    second_sum.finish(grad_second, scale)
    first_sum.finish(grad_first, scale)
    for pair in halos:
        for copy in pair:
            copy.wait_send()


def shards(features, cotangent, first_weight, second_weight, send_rows, gather_rows):
    scenes, bricks = lax.axis_size("scene"), lax.axis_size("brick")
    rows, cols = brick_grid(bricks)
    field = jax.ShapeDtypeStruct((VOX, C), jnp.bfloat16)
    grad = jax.ShapeDtypeStruct((TAPS * C, C), jnp.float32)
    even = pltpu.VMEM((SPAN, SPAN * EDGE, DEEP), jnp.bfloat16)
    odd = pltpu.VMEM((SPAN, VOX // EDGE, DEEP), jnp.bfloat16)
    spread = pltpu.VMEM((PAIRS, DEEP, LANES), jnp.bfloat16)
    halo = pltpu.VMEM((EXCHANGES, LANES, LANES), jnp.bfloat16)
    scratch = [
        pltpu.VMEM((EDGE, 1024), jnp.float32),
        pltpu.VMEM((1024, LANES), jnp.float32),
        pltpu.VMEM((3, SLAB, POOL), jnp.bfloat16),
        pltpu.VMEM((LANES, VOX), jnp.bfloat16),
        pltpu.VMEM((3, SLAB, LANES), jnp.float32),
        halo,
        halo,
        pltpu.SemaphoreType.DMA((EXCHANGES, 2)),
        pltpu.SemaphoreType.DMA((EXCHANGES, 2)),
        spread, spread, spread, spread,
        even, odd, even, odd, even, odd,
        pltpu.VMEM((VOX, LANES), jnp.float32),
    ]
    out, grad_in, grad_first, grad_second = pl.pallas_call(
        functools.partial(step_kernel, scenes, bricks),
        out_shape=(field, field, grad, grad),
        in_specs=[pl.BlockSpec(memory_space=pltpu.VMEM)] * 6,
        out_specs=[pl.BlockSpec(memory_space=pltpu.VMEM)] * 4,
        scratch_shapes=scratch + Reduction.scratch(scenes, rows, cols) * 2,
        compiler_params=pltpu.CompilerParams(
            collective_id=0, has_side_effects=True, vmem_limit_bytes=48 * 1024 * 1024
        ),
    )(features[0], cotangent[0], first_weight, second_weight, send_rows, gather_rows)
    return out[None], grad_in[None], grad_first, grad_second


def solution(mesh):
    in_specs = (
        P("scene", "brick", None),
        P("scene", "brick", None),
        P(),
        P(),
        P("scene", "brick"),
        P("scene", "brick"),
    )
    out_specs = (P("scene", "brick", None), P("scene", "brick", None), P(), P())
    return jax.shard_map(shards, mesh=mesh, in_specs=in_specs, out_specs=out_specs, check_vma=False)
```

time: 173 us -> 79 us (0.46); the launches traced: 171 us -> 78.8 us
  local copies, waits for them, and re-layouts: 58.9 us -> 7.14 us
  starting transfers between devices: 24 us -> 0 us
  matrix products: 20.3 us -> 0 us
  Pallas kernels: 53.4 us -> 71 us
  other arithmetic: 7.82 us -> 0 us
  waiting for transfers between devices: 4.87 us -> 0 us
    ppermute x8 -> x0, starting transfers between devices: 24 us -> none  [the longest x4 18.6 us: extended(): lax.ppermute(lax.slice_in_dim(block, block.shape[dim] - width, None, axis...]
    dot_general x54 -> x0, matrix products: 20.3 us -> none  [the longest x36 14 us: convolve(): jnp.dot(window_rows(padded, row_off, col_off, extent), weight[start:start...]
    pallas_call x1, Pallas kernels: 53.4 us -> 71 us  [shards(): pl.pallas_call(functools.partial(step_kernel, scenes, bricks), out_shape=...]
    unnamed x118 -> x16, local copies, waits for them, and re-layouts: 23.8 us -> 7.14 us
    gather x11 -> x0, local copies, waits for them, and re-layouts: 16.4 us -> none  [the longest x4 13.3 us: assemble(): jnp.take(pool, gather_list, axis=0)]
    slice x32 -> x0, local copies, waits for them, and re-layouts: 15.3 us -> none  [the longest x20 12.5 us: convolve(): weight[start:start + 3 * width]]
    concatenate x36 -> x0, other arithmetic: 5.55 us -> none  [the longest x32 5.14 us: window_rows(): return jnp.concatenate(slabs, axis=-1).reshape(-1, 3 * padded.shape[-1])]
    ppermute x8 -> x0, waiting for transfers between devices: 4.87 us -> none  [the longest x4 4.86 us: extended(): lax.ppermute(lax.slice_in_dim(block, 0, width, axis=dim), axis, backward)]
  transfers between devices with their start and end apart: 8 -> 0, of which waited for: 2 -> 0; matrix products, arithmetic and copies ran while one was open for 10% -> 0% of each run, Pallas kernels for 31% -> 0%
where the time goes in v2:
time: 79 us; the launch traced here: 78.8 us
  Pallas kernels  71 us (90%)
  local copies, waits for them, and re-layouts  7.14 us (9%)
    pallas_call x1, Pallas kernels, shards(): pl.pallas_call(functools.partial(step_kernel, scenes, bricks), out_shape=...  71 us
    unnamed x16, local copies, waits for them, and re-layouts  7.14 us

profile of v2, /device:TPU:1, one launch (start us, length us, event | category | flops | bytes accessed | tf_op | source)
XLA Modules:
  0.0 78.8 jit_solution(17817995595396225638)
XLA Ops:
  0.6 0.0 copy-start.2
  0.6 1.0 %copy.10 = bf16[1,512,64]{2,1,0:T(8,128)(2,1)S(1)} copy(bf16[1,512,64]{1,2,0:T(8,128)(2,1)} %param.6) | data formatting | bytes 131072 | tf_op args[0]
  1.6 1.0 %copy.11 = bf16[1,512,64]{2,1,0:T(8,128)(2,1)S(1)} copy(bf16[1,512,64]{1,2,0:T(8,128)(2,1)} %param.7) | data formatting | bytes 131072 | tf_op args[1]
  2.6 0.0 copy-done.2
  2.6 0.0 copy-start.3
  2.6 0.3 copy.12.first_weight
  2.9 0.7 copy-done.3
  3.6 0.0 copy-start
  3.6 0.0 copy-start.1
  3.6 0.3 copy.13.second_weight
  3.8 0.4 copy-done
  4.2 0.0 copy-done.1
  4.3 71.0 %shard_map.93 = (bf16[512,64]{1,0:T(8,128)(2,1)S(1)}, bf16[512,64]{1,0:T(8,128)(2,1)S(1)}, f32[1728,64]{1,0:T(8,128)S(1)}, f32[1728,64]{1,0:T(8,128)S(1)}) custom-call(bf16[512,64]{1,0:T(8,128)(2,1)S(1)} %bitcast.4, bf16[512,64]{1,0:T(8,128)(2,1)S(1)} %bitcast.5, bf16[1728,64]{1,0:T(8,128)(2,1)S(1)} %copy.12.first_weight, ...), custom_call_target="tpu_custom_call" | custom-call | tf_op jit(solution)/shard_map/pallas_call | solution.py:415
  75.2 0.7 copy.14
  75.9 0.7 copy.15
  76.7 1.1 %copy.16 = f32[1728,64]{0,1:T(8,128)} copy(f32[1728,64]{1,0:T(8,128)S(1)} %get-tuple-element.14) | data formatting | bytes 884736
  77.7 1.1 %copy.17 = f32[1728,64]{0,1:T(8,128)} copy(f32[1728,64]{1,0:T(8,128)S(1)} %get-tuple-element.15) | data formatting | bytes 884736
Async XLA Ops:
  0.6 2.0 %copy-start.2 = (bf16[1728,64]{0,1:T(8,128)(2,1)S(1)}, bf16[1728,64]{0,1:T(8,128)(2,1)}, u32[]{:S(2)}) copy-start(bf16[1728,64]{0,1:T(8,128)(2,1)} %param.8) | copy-start | bytes 663556
  2.6 0.9 %copy-start.3 = (bf16[1728,64]{0,1:T(8,128)(2,1)S(1)}, bf16[1728,64]{0,1:T(8,128)(2,1)}, u32[]{:S(2)}) copy-start(bf16[1728,64]{0,1:T(8,128)(2,1)} %param.9) | copy-start | bytes 663556
  3.6 0.7 copy-start
  3.6 0.7 copy-start.1

commit v3 on v2

--- a/solution.py
+++ b/solution.py
@@ -188,15 +188,9 @@
         self.arrive()
         everything = self.full[...].reshape(1024, LANES)
         for block in range(BLOCKS):
+            lanes = min(LANES, TAPS * C - block * LANES)
             piece = everything[block * C : (block + 1) * C].astype(jnp.float32) * scale
-            piece = jnp.transpose(piece)
-            if block < PAIRS:
-                out[pl.ds(block * 3 * C, 2 * C), :] = piece
-            else:
-                for half in range(2):
-                    pair = 2 * (block - PAIRS) + half
-                    if pair < PAIRS:
-                        out[pl.ds(pair * 3 * C + 2 * C, C), :] = piece[half * C : (half + 1) * C]
+            out[:, block * LANES : block * LANES + lanes] = piece[:, :lanes]
         for copy in self.started:
             copy.wait_send()
 
@@ -257,43 +251,68 @@
     held = None
     for pair in range(PAIRS):
         got = matmul(turned, field.window(pair))
-        put(pair, got[:, :LANES].astype(jnp.bfloat16))
-        last = got[:, LANES:]
+        first, last = got[:, :LANES], got[:, LANES:]
+        block = 3 * (pair // 2)
         if pair % 2 == 0:
+            put(block, first.astype(jnp.bfloat16))
             held = last
         else:
-            put(PAIRS + pair // 2, jnp.where(low, held, last).astype(jnp.bfloat16))
-    put(PAIRS + PAIRS // 2, held.astype(jnp.bfloat16))
+            first = jnp.concatenate([first[:, C:], first[:, :C]], axis=1)
+            put(block + 1, jnp.where(low, held, first).astype(jnp.bfloat16))
+            put(block + 2, jnp.where(low, first, last).astype(jnp.bfloat16))
+    put(BLOCKS - 1, held.astype(jnp.bfloat16))
+
+
+def upright(turned):
+    return jnp.transpose(jnp.concatenate([turned, turned], axis=0))
 
 
 def spread_weight(weight, plain, flip):
     zero = jnp.zeros((C, LANES), jnp.bfloat16)
     for pair in range(PAIRS):
-        plain[pair, : 3 * C, :] = twice(weight[pl.ds(pair * 3 * C, 3 * C), :])
         plain[pair, 3 * C :, :] = zero
         flip[pair, 3 * C :, :] = zero
-        for c in range(3):
-            source = (TAPS - 1 - (3 * pair + c)) * C
-            block = twice(weight[pl.ds(source, C), :].astype(jnp.float32))
-            block = jnp.transpose(block)[:C]
-            block = twice(block)
-            flip[pair, c * C : (c + 1) * C, :] = block.astype(jnp.bfloat16)
+    for at in range(0, TAPS, 2):
+        taps = min(2, TAPS - at)
+        stood = upright(weight[:, at * C : (at + taps) * C])
+        for tap in range(at, at + taps):
+            pair, c = tap // 3, tap % 3
+            plain[pair, c * C : (c + 1) * C, :] = stood[(tap - at) * C : (tap - at + 1) * C]
+            pair, c = (TAPS - 1 - tap) // 3, (TAPS - 1 - tap) % 3
+            flip[pair, c * C : (c + 1) * C, :] = twice(weight[:, tap * C : (tap + 1) * C])
 
 
 def step_kernel(
-    scenes, bricks, features, cotangent, first_weight, second_weight, send_rows, gather_rows,
-    output, grad_input, grad_first, grad_second,
+    scenes, bricks, features_in, cotangent_in, first_weight_in, second_weight_in, send_in, gather_in,
+    output_out, grad_input_out, grad_first_out, grad_second_out,
+    output, grad_input, grad_first, grad_second, store_sems,
+    features, cotangent, first_weight, second_weight, send_rows, gather_rows, load_sems,
     indices, columns, gather_hot, send_hot, pads, halo_out, halo_in, halo_send, halo_recv,
     first_plain, first_flip, second_plain, second_flip,
     even_in, odd_in, even_act, odd_act, even_delta, odd_delta, first_pre_ref, *reduction,
 ):
     pos = Position(scenes, bricks)
     peers = [pos.down_id(), pos.up_id()] + pos.reduce_peers()
+    loads = [
+        pltpu.make_async_copy(source, target, load_sems.at[at])
+        for at, (source, target) in enumerate((
+            (send_in, send_rows), (features_in, features), (gather_in, gather_rows),
+            (first_weight_in, first_weight), (second_weight_in, second_weight),
+            (cotangent_in, cotangent),
+        ))
+    ]
+    for load in loads:
+        load.start()
     greet(peers)
     half = len(reduction) // 2
     first_sum = Reduction(pos, reduction[:half])
     second_sum = Reduction(pos, reduction[half:])
     halos = []
+    stores = []
+
+    def store(source, target):
+        stores.append(pltpu.make_async_copy(source, target, store_sems.at[len(stores)]))
+        stores[-1].start()
 
     def send_halo(values):
         at = len(halos)
@@ -319,9 +338,12 @@
             pads[c] = pads[c] + matmul(gather_hot[c, :, VOX:], rows)
         field.fill([pads.at[c] for c in range(3)])
 
+    loads[0].wait()
     send_hot[...] = hot(as_columns(send_rows[...].astype(jnp.float32)), VOX)
-    feature_rows = twice(features[...])
+    loads[1].wait()
+    feature_rows = upright(features[...])
     send_halo(feature_rows)
+    loads[2].wait()
 
     indices[...] = jnp.full(indices.shape, float(POOL), jnp.float32)
     indices[:, :CELLS] = jnp.broadcast_to(gather_rows[...].astype(jnp.float32), (EDGE, CELLS))
@@ -333,12 +355,16 @@
         )
         gather_hot[c] = hot(taken, POOL)
     gather_local(feature_rows)
+    loads[3].wait()
     spread_weight(first_weight, first_plain, first_flip)
+    loads[4].wait()
     spread_weight(second_weight, second_plain, second_flip)
     for one in (first_sum, second_sum):
         for block in (BLOCKS, BLOCKS + 1):
             one.put(block, jnp.zeros((C, LANES), jnp.bfloat16))
 
+    loads[5].wait()
+    cot = upright(cotangent[...]).astype(jnp.float32)
     field_in = Field(even_in, odd_in)
     field_act = Field(even_act, odd_act)
     field_delta = Field(even_delta, odd_delta)
@@ -353,10 +379,11 @@
     second_pre = field_act.conv(second_plain)
     sig = jax.nn.sigmoid(second_pre)
     slope = sig * (1.0 + second_pre * (1.0 - sig))
-    second_delta32 = twice(cotangent[...]).astype(jnp.float32) * slope
+    second_delta32 = cot * slope
     second_delta = second_delta32.astype(jnp.bfloat16)
     send_halo(second_delta)
-    output[...] = (second_pre * sig).astype(jnp.bfloat16)[:, :C]
+    output[...] = jnp.transpose(second_pre * sig)[:C].astype(jnp.bfloat16)
+    store(output, output_out)
     weight_gradient(field_act, second_delta32, second_sum.put)
     second_sum.start_scene()
     gather_local(second_delta)
@@ -375,7 +402,8 @@
     gather_halo(field_delta)
     second_sum.start_col()
     first_sum.start_row()
-    grad_input[...] = field_delta.conv(first_flip).astype(jnp.bfloat16)[:, :C]
+    grad_input[...] = jnp.transpose(field_delta.conv(first_flip))[:C].astype(jnp.bfloat16)
+    store(grad_input, grad_input_out)
     second_sum.start_row_back()
     first_sum.start_col()
     second_sum.start_scene_back()
@@ -383,22 +411,45 @@
     first_sum.start_scene_back()
     scale = float(scenes * bricks * VOX) ** (-0.5)
     second_sum.finish(grad_second, scale)
+    store(grad_second, grad_second_out)
     first_sum.finish(grad_first, scale)
+    store(grad_first, grad_first_out)
+    for copy in stores:
+        copy.wait()
     for pair in halos:
         for copy in pair:
             copy.wait_send()
 
 
+def hand_over(*refs):
+    count = 4
+    sources, targets, held = refs[:count], refs[count : 2 * count], refs[2 * count : 3 * count]
+    load_sems, store_sems = refs[3 * count :]
+    loads = [pltpu.make_async_copy(sources[at], held[at], load_sems.at[at]) for at in range(count)]
+    stores = [pltpu.make_async_copy(held[at], targets[at], store_sems.at[at]) for at in range(count)]
+    for load in loads:
+        load.start()
+    for load, store in zip(loads, stores):
+        load.wait()
+        store.start()
+    for store in stores:
+        store.wait()
+
+
 def shards(features, cotangent, first_weight, second_weight, send_rows, gather_rows):
     scenes, bricks = lax.axis_size("scene"), lax.axis_size("brick")
     rows, cols = brick_grid(bricks)
-    field = jax.ShapeDtypeStruct((VOX, C), jnp.bfloat16)
-    grad = jax.ShapeDtypeStruct((TAPS * C, C), jnp.float32)
+    field = jax.ShapeDtypeStruct((C, VOX), jnp.bfloat16)
+    grad = jax.ShapeDtypeStruct((C, TAPS * C), jnp.float32)
+    operands = [features[0].T, cotangent[0].T, first_weight.T, second_weight.T, send_rows, gather_rows]
     even = pltpu.VMEM((SPAN, SPAN * EDGE, DEEP), jnp.bfloat16)
     odd = pltpu.VMEM((SPAN, VOX // EDGE, DEEP), jnp.bfloat16)
     spread = pltpu.VMEM((PAIRS, DEEP, LANES), jnp.bfloat16)
     halo = pltpu.VMEM((EXCHANGES, LANES, LANES), jnp.bfloat16)
-    scratch = [
+    results = [pltpu.VMEM(one.shape, one.dtype) for one in (field, field, grad, grad)]
+    results.append(pltpu.SemaphoreType.DMA((4,)))
+    scratch = results + [pltpu.VMEM(one.shape, one.dtype) for one in operands] + [
+        pltpu.SemaphoreType.DMA((len(operands),)),
         pltpu.VMEM((EDGE, 1024), jnp.float32),
         pltpu.VMEM((1024, LANES), jnp.float32),
         pltpu.VMEM((3, SLAB, POOL), jnp.bfloat16),
@@ -415,14 +466,22 @@
     out, grad_in, grad_first, grad_second = pl.pallas_call(
         functools.partial(step_kernel, scenes, bricks),
         out_shape=(field, field, grad, grad),
-        in_specs=[pl.BlockSpec(memory_space=pltpu.VMEM)] * 6,
-        out_specs=[pl.BlockSpec(memory_space=pltpu.VMEM)] * 4,
+        in_specs=[pl.BlockSpec(memory_space=pltpu.HBM)] * 6,
+        out_specs=[pl.BlockSpec(memory_space=pltpu.HBM)] * 4,
         scratch_shapes=scratch + Reduction.scratch(scenes, rows, cols) * 2,
         compiler_params=pltpu.CompilerParams(
-            collective_id=0, has_side_effects=True, vmem_limit_bytes=48 * 1024 * 1024
+            collective_id=0, has_side_effects=True, vmem_limit_bytes=62 * 1024 * 1024
         ),
-    )(features[0], cotangent[0], first_weight, second_weight, send_rows, gather_rows)
-    return out[None], grad_in[None], grad_first, grad_second
+    )(*operands)
+    out, grad_in, grad_first, grad_second = pl.pallas_call(
+        hand_over,
+        out_shape=(field, field, grad, grad),
+        in_specs=[pl.BlockSpec(memory_space=pltpu.HBM)] * 4,
+        out_specs=[pl.BlockSpec(memory_space=pltpu.HBM)] * 4,
+        scratch_shapes=results[:4] + [pltpu.SemaphoreType.DMA((4,))] * 2,
+        compiler_params=pltpu.CompilerParams(vmem_limit_bytes=62 * 1024 * 1024),
+    )(out, grad_in, grad_first, grad_second)
+    return out.T[None], grad_in.T[None], grad_first.T, grad_second.T
 
 
 def solution(mesh):

time: 79 us -> 70.1 us (0.89)
  local copies, waits for them, and re-layouts: 7.14 us -> 0 us
  Pallas kernels: 71 us -> 69.3 us
    unnamed x16 -> x0, local copies, waits for them, and re-layouts: 7.14 us -> none
    pallas_call x1, Pallas kernels: 71 us -> 67.2 us  [shards(): pl.pallas_call(functools.partial(step_kernel, scenes, bricks), out_shape=...]
    pallas_call x0 -> x1, Pallas kernels: none -> 2.08 us  [shards(): pl.pallas_call(hand_over, out_shape=(field, field, grad, grad), in_specs=...]
where the time goes in v3:
time: 70.1 us; the launch traced here: 69.9 us
  Pallas kernels  69.3 us (99%)
    pallas_call x1, Pallas kernels, shards(): pl.pallas_call(functools.partial(step_kernel, scenes, bricks), out_shape=...  67.2 us
    pallas_call x1, Pallas kernels, shards(): pl.pallas_call(hand_over, out_shape=(field, field, grad, grad), in_specs=...  2.08 us

profile of v3, /device:TPU:1, one launch (start us, length us, event | category | flops | bytes accessed | tf_op | source)
XLA Modules:
  0.0 69.9 jit_solution(15251493832340596310)
XLA Ops:
  0.6 67.2 %shard_map.93 = (bf16[64,512]{1,0:T(8,128)(2,1)}, bf16[64,512]{1,0:T(8,128)(2,1)}, f32[64,1728]{1,0:T(8,128)}, f32[64,1728]{1,0:T(8,128)}) custom-call(bf16[64,512]{1,0:T(8,128)(2,1)} %bitcast.18, bf16[64,512]{1,0:T(8,128)(2,1)} %bitcast.19, bf16[64,1728]{1,0:T(8,128)(2,1)} %bitcast.16, bf16[64,1728]{1,0:T(8,128)(2,1)} %bitcast.17, s32[1,128]{1,0:T(1,128)} %send_in.1, ...), custom_call_target="tpu_custom_call" | custom-call | tf_op jit(solution)/shard_map/pallas_call | solution.py:466
  67.8 2.1 %shard_map.94 = (bf16[64,512]{1,0:T(8,128)(2,1)}, bf16[64,512]{1,0:T(8,128)(2,1)}, f32[64,1728]{1,0:T(8,128)}, f32[64,1728]{1,0:T(8,128)}) custom-call(bf16[64,512]{1,0:T(8,128)(2,1)} %get-tuple-element.12.refs_0_, bf16[64,512]{1,0:T(8,128)(2,1)} %get-tuple-element.13.refs_1_, f32[64,1728]{1,0:T(8,128)} %get-tuple-element.14.refs_2_, ...), custom_call_target="tpu_custom_call" | custom-call | tf_op jit(solution)/shard_map/pallas_call | solution.py:476

commit v4 on v3

--- a/solution.py
+++ b/solution.py
@@ -28,6 +28,10 @@
         if count % rows == 0 and count // rows > 1:
             return rows, count // rows
     return 1, count
+
+
+def far_first(count):
+    return sorted(range(1, count), key=lambda step: (-min(step, count - step), step))
 
 
 class Position:
@@ -126,10 +130,12 @@
             ]
 
     def send(self, which, src, dst, peers):
-        self.current = []
-        for k, (peer, s, d) in enumerate(zip(peers, src, dst)):
-            sems = self.sems[which]
-            self.current.append(remote(s, d, sems[0].at[k], sems[1].at[k], peer))
+        sems = self.sems[which]
+        self.current = [
+            remote(src[step - 1], dst[step - 1], sems[0].at[step - 1], sems[1].at[step - 1],
+                   peers[step - 1])
+            for step in far_first(len(peers) + 1)
+        ]
         self.started += self.current
 
     def arrive(self):
@@ -229,20 +235,28 @@
             rows = self.even[a : a + EDGE, EDGE * b : EDGE * b + VOX // EDGE]
         return rows.reshape(VOX, DEEP)
 
-    def fill(self, pads):
+    def fill(self, pads, halo_hot, rows):
         low = lax.broadcasted_iota(jnp.int32, (1, LANES), 1) < C
-        first = jnp.where(low, pads[0][...], pads[1][...]).reshape(SPAN, SPAN * EDGE, LANES)
-        last = pads[2][...].reshape(SPAN, SPAN * EDGE, LANES)
-        odd = slice(EDGE, EDGE + VOX // EDGE)
-        for at, part in ((0, first), (LANES, last)):
-            self.even[:, :, at : at + LANES] = part.astype(jnp.bfloat16)
-            self.odd[:, :, at : at + LANES] = part[:, odd].astype(jnp.bfloat16)
+        for plane in range(0, SPAN, 2):
+            span = slice(plane * SPAN * EDGE, (plane + 2) * SPAN * EDGE)
+            cells = [pads[c, span] + matmul(halo_hot[c, span, VOX:], rows) for c in range(3)]
+            for lane, values in ((0, jnp.where(low, cells[0], cells[1])), (LANES, cells[2])):
+                for half in range(2):
+                    part = values[half * SPAN * EDGE : (half + 1) * SPAN * EDGE]
+                    self.even[plane + half, :, lane : lane + LANES] = part.astype(jnp.bfloat16)
+                    self.odd[plane + half, :, lane : lane + LANES] = part[
+                        EDGE : EDGE + VOX // EDGE
+                    ].astype(jnp.bfloat16)
 
     def conv(self, weight):
-        total = matmul(self.window(0), weight[0])
-        for pair in range(1, PAIRS):
-            total = total + matmul(self.window(pair), weight[pair])
-        return total
+        rows = VOX // 2
+        parts = []
+        for at in range(2):
+            total = matmul(self.window(0)[at * rows : (at + 1) * rows], weight[0])
+            for pair in range(1, PAIRS):
+                total = total + matmul(self.window(pair)[at * rows : (at + 1) * rows], weight[pair])
+            parts.append(total)
+        return jnp.concatenate(parts, axis=0)
 
 
 def weight_gradient(field, delta, put):
@@ -267,19 +281,23 @@
     return jnp.transpose(jnp.concatenate([turned, turned], axis=0))
 
 
-def spread_weight(weight, plain, flip):
-    zero = jnp.zeros((C, LANES), jnp.bfloat16)
+def spread_plain(weight, plain):
     for pair in range(PAIRS):
-        plain[pair, 3 * C :, :] = zero
-        flip[pair, 3 * C :, :] = zero
+        plain[pair, 3 * C :, :] = jnp.zeros((C, LANES), jnp.bfloat16)
     for at in range(0, TAPS, 2):
         taps = min(2, TAPS - at)
         stood = upright(weight[:, at * C : (at + taps) * C])
         for tap in range(at, at + taps):
             pair, c = tap // 3, tap % 3
             plain[pair, c * C : (c + 1) * C, :] = stood[(tap - at) * C : (tap - at + 1) * C]
-            pair, c = (TAPS - 1 - tap) // 3, (TAPS - 1 - tap) % 3
-            flip[pair, c * C : (c + 1) * C, :] = twice(weight[:, tap * C : (tap + 1) * C])
+
+
+def spread_flip(weight, flip):
+    for pair in range(PAIRS):
+        flip[pair, 3 * C :, :] = jnp.zeros((C, LANES), jnp.bfloat16)
+    for tap in range(TAPS):
+        pair, c = (TAPS - 1 - tap) // 3, (TAPS - 1 - tap) % 3
+        flip[pair, c * C : (c + 1) * C, :] = twice(weight[:, tap * C : (tap + 1) * C])
 
 
 def step_kernel(
@@ -289,7 +307,7 @@
     features, cotangent, first_weight, second_weight, send_rows, gather_rows, load_sems,
     indices, columns, gather_hot, send_hot, pads, halo_out, halo_in, halo_send, halo_recv,
     first_plain, first_flip, second_plain, second_flip,
-    even_in, odd_in, even_act, odd_act, even_delta, odd_delta, first_pre_ref, *reduction,
+    even_in, odd_in, even_act, odd_act, even_delta, odd_delta, first_slope, *reduction,
 ):
     pos = Position(scenes, bricks)
     peers = [pos.down_id(), pos.up_id()] + pos.reduce_peers()
@@ -327,22 +345,20 @@
 
     def gather_local(values):
         for c in range(3):
-            pads[c] = matmul(gather_hot[c, :, :VOX], values)
+            for at in range(0, SLAB, 160):
+                pads[c, at : at + 160] = matmul(gather_hot[c, at : at + 160, :VOX], values)
 
     def gather_halo(field):
         at = len(halos) - 1
         for copy in halos[at]:
             copy.wait_recv()
         rows = halo_in[at]
-        for c in range(3):
-            pads[c] = pads[c] + matmul(gather_hot[c, :, VOX:], rows)
-        field.fill([pads.at[c] for c in range(3)])
+        field.fill(pads, gather_hot, rows)
 
     loads[0].wait()
     send_hot[...] = hot(as_columns(send_rows[...].astype(jnp.float32)), VOX)
     loads[1].wait()
     feature_rows = upright(features[...])
-    send_halo(feature_rows)
     loads[2].wait()
 
     indices[...] = jnp.full(indices.shape, float(POOL), jnp.float32)
@@ -354,27 +370,29 @@
             [columns[pl.ds(SPAN * row + c, EDGE), :] for row in range(SPAN * SPAN)], axis=0
         )
         gather_hot[c] = hot(taken, POOL)
+    send_halo(feature_rows)
     gather_local(feature_rows)
     loads[3].wait()
-    spread_weight(first_weight, first_plain, first_flip)
-    loads[4].wait()
-    spread_weight(second_weight, second_plain, second_flip)
+    spread_plain(first_weight, first_plain)
     for one in (first_sum, second_sum):
         for block in (BLOCKS, BLOCKS + 1):
             one.put(block, jnp.zeros((C, LANES), jnp.bfloat16))
 
-    loads[5].wait()
-    cot = upright(cotangent[...]).astype(jnp.float32)
     field_in = Field(even_in, odd_in)
     field_act = Field(even_act, odd_act)
     field_delta = Field(even_delta, odd_delta)
 
     gather_halo(field_in)
     first_pre = field_in.conv(first_plain)
-    first_pre_ref[...] = first_pre
-    first_act = (first_pre * jax.nn.sigmoid(first_pre)).astype(jnp.bfloat16)
+    sig = jax.nn.sigmoid(first_pre)
+    first_act = (first_pre * sig).astype(jnp.bfloat16)
     send_halo(first_act)
     gather_local(first_act)
+    first_slope[...] = sig * (1.0 + first_pre * (1.0 - sig))
+    loads[4].wait()
+    spread_plain(second_weight, second_plain)
+    loads[5].wait()
+    cot = upright(cotangent[...]).astype(jnp.float32)
     gather_halo(field_act)
     second_pre = field_act.conv(second_plain)
     sig = jax.nn.sigmoid(second_pre)
@@ -382,30 +400,28 @@
     second_delta32 = cot * slope
     second_delta = second_delta32.astype(jnp.bfloat16)
     send_halo(second_delta)
-    output[...] = jnp.transpose(second_pre * sig)[:C].astype(jnp.bfloat16)
-    store(output, output_out)
     weight_gradient(field_act, second_delta32, second_sum.put)
     second_sum.start_scene()
     gather_local(second_delta)
+    spread_flip(second_weight, second_flip)
+    output[...] = jnp.transpose(second_pre * sig)[:C].astype(jnp.bfloat16)
+    store(output, output_out)
     gather_halo(field_delta)
-    first_back = field_delta.conv(second_flip)
-    first_pre = first_pre_ref[...]
-    sig = jax.nn.sigmoid(first_pre)
-    slope = sig * (1.0 + first_pre * (1.0 - sig))
-    first_delta32 = first_back * slope
+    first_delta32 = field_delta.conv(second_flip) * first_slope[...]
+    weight_gradient(field_in, first_delta32, first_sum.put)
+    first_sum.start_scene()
     first_delta = first_delta32.astype(jnp.bfloat16)
     send_halo(first_delta)
-    weight_gradient(field_in, first_delta32, first_sum.put)
-    first_sum.start_scene()
+    spread_flip(first_weight, first_flip)
+    gather_local(first_delta)
     second_sum.start_row()
-    gather_local(first_delta)
     gather_halo(field_delta)
     second_sum.start_col()
     first_sum.start_row()
     grad_input[...] = jnp.transpose(field_delta.conv(first_flip))[:C].astype(jnp.bfloat16)
     store(grad_input, grad_input_out)
+    first_sum.start_col()
     second_sum.start_row_back()
-    first_sum.start_col()
     second_sum.start_scene_back()
     first_sum.start_row_back()
     first_sum.start_scene_back()

time: 70.1 us -> 65.3 us (0.932)
  Pallas kernels: 69.3 us -> 64.4 us
    pallas_call x1, Pallas kernels: 67.2 us -> 62.4 us  [shards(): pl.pallas_call(functools.partial(step_kernel, scenes, bricks), out_shape=...]
where the time goes in v4:
time: 65.3 us; the launch traced here: 65.1 us
  Pallas kernels  64.4 us (99%)
    pallas_call x1, Pallas kernels, shards(): pl.pallas_call(functools.partial(step_kernel, scenes, bricks), out_shape=...  62.4 us
    pallas_call x1, Pallas kernels, shards(): pl.pallas_call(hand_over, out_shape=(field, field, grad, grad), in_specs=...  2.08 us

profile of v4, /device:TPU:1, one launch (start us, length us, event | category | flops | bytes accessed | tf_op | source)
XLA Modules:
  0.0 65.1 jit_solution(12840469550127877700)
XLA Ops:
  0.6 62.4 %shard_map.93 = (bf16[64,512]{1,0:T(8,128)(2,1)}, bf16[64,512]{1,0:T(8,128)(2,1)}, f32[64,1728]{1,0:T(8,128)}, f32[64,1728]{1,0:T(8,128)}) custom-call(bf16[64,512]{1,0:T(8,128)(2,1)} %bitcast.18, bf16[64,512]{1,0:T(8,128)(2,1)} %bitcast.19, bf16[64,1728]{1,0:T(8,128)(2,1)} %bitcast.16, bf16[64,1728]{1,0:T(8,128)(2,1)} %bitcast.17, s32[1,128]{1,0:T(1,128)} %send_in.1, ...), custom_call_target="tpu_custom_call" | custom-call | tf_op jit(solution)/shard_map/pallas_call | solution.py:482
  63.0 2.1 %shard_map.94 = (bf16[64,512]{1,0:T(8,128)(2,1)}, bf16[64,512]{1,0:T(8,128)(2,1)}, f32[64,1728]{1,0:T(8,128)}, f32[64,1728]{1,0:T(8,128)}) custom-call(bf16[64,512]{1,0:T(8,128)(2,1)} %get-tuple-element.12.refs_0_, bf16[64,512]{1,0:T(8,128)(2,1)} %get-tuple-element.13.refs_1_, f32[64,1728]{1,0:T(8,128)} %get-tuple-element.14.refs_2_, ...), custom_call_target="tpu_custom_call" | custom-call | tf_op jit(solution)/shard_map/pallas_call | solution.py:492

commit v5 on v4

--- a/solution.py
+++ b/solution.py
@@ -68,11 +68,33 @@
     def up_id(self):
         return (self.scene, lax.rem(self.brick + 1, self.bricks))
 
-    def reduce_peers(self):
-        peers = [self.scene_id(k) for k in range(1, self.scenes)]
-        peers += [self.row_id(k) for k in range(1, self.rows)]
-        peers += [self.col_id(k) for k in range(1, self.cols)]
-        return peers
+    def near_peers(self):
+        peers = [self.down_id(), self.up_id()] + self.row_pair(1) + self.col_pair(1)
+        return peers + [self.scene_id(k) for k in far_first(self.scenes)]
+
+    def row_pair(self, step):
+        return [self.row_id(step), self.row_id(self.rows - step)]
+
+    def col_pair(self, step):
+        return [self.col_id(step), self.col_id(self.cols - step)]
+
+
+class Word:
+    def __init__(self, pos, sems):
+        self.rounds = [
+            [(sems.at[0], pos.col_pair(1)), (sems.at[1], pos.row_pair(1))],
+            [(sems.at[2], pos.col_pair(2)), (sems.at[3], pos.row_pair(2))],
+            [(sems.at[4], pos.col_pair(4))],
+        ]
+
+    def give(self, at):
+        for sem, peers in self.rounds[at]:
+            for peer in peers:
+                pl.semaphore_signal(sem, inc=1, device_id=peer, device_id_type=MESH)
+
+    def take(self, at):
+        for sem, peers in self.rounds[at]:
+            pl.semaphore_wait(sem, len(peers))
 
 
 def greet(peers):
@@ -307,10 +329,11 @@
     features, cotangent, first_weight, second_weight, send_rows, gather_rows, load_sems,
     indices, columns, gather_hot, send_hot, pads, halo_out, halo_in, halo_send, halo_recv,
     first_plain, first_flip, second_plain, second_flip,
-    even_in, odd_in, even_act, odd_act, even_delta, odd_delta, first_slope, *reduction,
+    even_in, odd_in, even_act, odd_act, even_delta, odd_delta, first_slope, word_sems, *reduction,
 ):
     pos = Position(scenes, bricks)
-    peers = [pos.down_id(), pos.up_id()] + pos.reduce_peers()
+    peers = pos.near_peers()
+    word = Word(pos, word_sems)
     loads = [
         pltpu.make_async_copy(source, target, load_sems.at[at])
         for at, (source, target) in enumerate((
@@ -359,6 +382,9 @@
     send_hot[...] = hot(as_columns(send_rows[...].astype(jnp.float32)), VOX)
     loads[1].wait()
     feature_rows = upright(features[...])
+    send_halo(feature_rows)
+    word.give(0)
+
     loads[2].wait()
 
     indices[...] = jnp.full(indices.shape, float(POOL), jnp.float32)
@@ -370,7 +396,6 @@
             [columns[pl.ds(SPAN * row + c, EDGE), :] for row in range(SPAN * SPAN)], axis=0
         )
         gather_hot[c] = hot(taken, POOL)
-    send_halo(feature_rows)
     gather_local(feature_rows)
     loads[3].wait()
     spread_plain(first_weight, first_plain)
@@ -383,6 +408,8 @@
     field_delta = Field(even_delta, odd_delta)
 
     gather_halo(field_in)
+    word.take(0)
+    word.give(1)
     first_pre = field_in.conv(first_plain)
     sig = jax.nn.sigmoid(first_pre)
     first_act = (first_pre * sig).astype(jnp.bfloat16)
@@ -394,6 +421,8 @@
     loads[5].wait()
     cot = upright(cotangent[...]).astype(jnp.float32)
     gather_halo(field_act)
+    word.take(1)
+    word.give(2)
     second_pre = field_act.conv(second_plain)
     sig = jax.nn.sigmoid(second_pre)
     slope = sig * (1.0 + second_pre * (1.0 - sig))
@@ -407,6 +436,7 @@
     output[...] = jnp.transpose(second_pre * sig)[:C].astype(jnp.bfloat16)
     store(output, output_out)
     gather_halo(field_delta)
+    word.take(2)
     first_delta32 = field_delta.conv(second_flip) * first_slope[...]
     weight_gradient(field_in, first_delta32, first_sum.put)
     first_sum.start_scene()
@@ -478,6 +508,7 @@
         spread, spread, spread, spread,
         even, odd, even, odd, even, odd,
         pltpu.VMEM((VOX, LANES), jnp.float32),
+        pltpu.SemaphoreType.REGULAR((5,)),
     ]
     out, grad_in, grad_first, grad_second = pl.pallas_call(
         functools.partial(step_kernel, scenes, bricks),

time: 65.3 us -> 64.4 us (0.986)
  Pallas kernels: 64.4 us -> 63.6 us
    pallas_call x1, Pallas kernels: 62.4 us -> 61.5 us  [shards(): pl.pallas_call(functools.partial(step_kernel, scenes, bricks), out_shape=...]
where the time goes in v5:
time: 64.4 us; the launch traced here: 64.3 us
  Pallas kernels  63.6 us (99%)
    pallas_call x1, Pallas kernels, shards(): pl.pallas_call(functools.partial(step_kernel, scenes, bricks), out_shape=...  61.5 us
    pallas_call x1, Pallas kernels, shards(): pl.pallas_call(hand_over, out_shape=(field, field, grad, grad), in_specs=...  2.08 us

profile of v5, /device:TPU:1, one launch (start us, length us, event | category | flops | bytes accessed | tf_op | source)
XLA Modules:
  0.0 64.3 jit_solution(5832008932289410439)
XLA Ops:
  0.6 61.5 %shard_map.93 = (bf16[64,512]{1,0:T(8,128)(2,1)}, bf16[64,512]{1,0:T(8,128)(2,1)}, f32[64,1728]{1,0:T(8,128)}, f32[64,1728]{1,0:T(8,128)}) custom-call(bf16[64,512]{1,0:T(8,128)(2,1)} %bitcast.18, bf16[64,512]{1,0:T(8,128)(2,1)} %bitcast.19, bf16[64,1728]{1,0:T(8,128)(2,1)} %bitcast.16, bf16[64,1728]{1,0:T(8,128)(2,1)} %bitcast.17, s32[1,128]{1,0:T(1,128)} %send_in.1, ...), custom_call_target="tpu_custom_call" | custom-call | tf_op jit(solution)/shard_map/pallas_call | solution.py:513
  62.2 2.1 %shard_map.94 = (bf16[64,512]{1,0:T(8,128)(2,1)}, bf16[64,512]{1,0:T(8,128)(2,1)}, f32[64,1728]{1,0:T(8,128)}, f32[64,1728]{1,0:T(8,128)}) custom-call(bf16[64,512]{1,0:T(8,128)(2,1)} %get-tuple-element.12.refs_0_, bf16[64,512]{1,0:T(8,128)(2,1)} %get-tuple-element.13.refs_1_, f32[64,1728]{1,0:T(8,128)} %get-tuple-element.14.refs_2_, ...), custom_call_target="tpu_custom_call" | custom-call | tf_op jit(solution)/shard_map/pallas_call | solution.py:523

commit v6 on v5

--- a/solution.py
+++ b/solution.py
@@ -468,13 +468,19 @@
 
 
 def hand_over(*refs):
-    count = 4
-    sources, targets, held = refs[:count], refs[count : 2 * count], refs[2 * count : 3 * count]
-    load_sems, store_sems = refs[3 * count :]
-    loads = [pltpu.make_async_copy(sources[at], held[at], load_sems.at[at]) for at in range(count)]
-    stores = [pltpu.make_async_copy(held[at], targets[at], store_sems.at[at]) for at in range(count)]
-    for load in loads:
-        load.start()
+    sources, targets, held = refs[:4], refs[4:8], refs[8:12]
+    load_sems, store_sems = refs[12:]
+    loads, stores = [], []
+    for at in (2, 3, 0, 1):
+        rows = held[at].shape[0] // 4 if at > 1 else held[at].shape[0]
+        for start in range(0, held[at].shape[0], rows):
+            part = pl.ds(start, rows)
+            sem = len(loads)
+            loads.append(pltpu.make_async_copy(
+                sources[at].at[part], held[at].at[part], load_sems.at[sem]))
+            stores.append(pltpu.make_async_copy(
+                held[at].at[part], targets[at].at[part], store_sems.at[sem]))
+            loads[-1].start()
     for load, store in zip(loads, stores):
         load.wait()
         store.start()
@@ -525,7 +531,7 @@
         out_shape=(field, field, grad, grad),
         in_specs=[pl.BlockSpec(memory_space=pltpu.HBM)] * 4,
         out_specs=[pl.BlockSpec(memory_space=pltpu.HBM)] * 4,
-        scratch_shapes=results[:4] + [pltpu.SemaphoreType.DMA((4,))] * 2,
+        scratch_shapes=results[:4] + [pltpu.SemaphoreType.DMA((10,))] * 2,
         compiler_params=pltpu.CompilerParams(vmem_limit_bytes=62 * 1024 * 1024),
     )(out, grad_in, grad_first, grad_second)
     return out.T[None], grad_in.T[None], grad_first.T, grad_second.T

time: 64.4 us -> 64.5 us (level)
  no operation moved by 1% of the time
where the time goes in v6:
time: 64.5 us; the launch traced here: 64.3 us
  Pallas kernels  63.7 us (99%)
    pallas_call x1, Pallas kernels, shards(): pl.pallas_call(functools.partial(step_kernel, scenes, bricks), out_shape=...  61.5 us
    pallas_call x1, Pallas kernels, shards(): pl.pallas_call(hand_over, out_shape=(field, field, grad, grad), in_specs=...  2.12 us

profile of v6, /device:TPU:1, one launch (start us, length us, event | category | flops | bytes accessed | tf_op | source)
XLA Modules:
  0.0 64.3 jit_solution(2403669269157095116)
XLA Ops:
  0.6 61.5 %shard_map.93 = (bf16[64,512]{1,0:T(8,128)(2,1)}, bf16[64,512]{1,0:T(8,128)(2,1)}, f32[64,1728]{1,0:T(8,128)}, f32[64,1728]{1,0:T(8,128)}) custom-call(bf16[64,512]{1,0:T(8,128)(2,1)} %bitcast.18, bf16[64,512]{1,0:T(8,128)(2,1)} %bitcast.19, bf16[64,1728]{1,0:T(8,128)(2,1)} %bitcast.16, bf16[64,1728]{1,0:T(8,128)(2,1)} %bitcast.17, s32[1,128]{1,0:T(1,128)} %send_in.1, ...), custom_call_target="tpu_custom_call" | custom-call | tf_op jit(solution)/shard_map/pallas_call | solution.py:519
  62.2 2.1 %shard_map.94 = (bf16[64,512]{1,0:T(8,128)(2,1)}, bf16[64,512]{1,0:T(8,128)(2,1)}, f32[64,1728]{1,0:T(8,128)}, f32[64,1728]{1,0:T(8,128)}) custom-call(bf16[64,512]{1,0:T(8,128)(2,1)} %get-tuple-element.12.refs_0_, bf16[64,512]{1,0:T(8,128)(2,1)} %get-tuple-element.13.refs_1_, f32[64,1728]{1,0:T(8,128)} %get-tuple-element.14.refs_2_, ...), custom_call_target="tpu_custom_call" | custom-call | tf_op jit(solution)/shard_map/pallas_call | solution.py:529
